TPU v7x, 32 devices: a whole 2x2x4 slice. The times are simulated.
32 devices in a mesh: row: 4 (over x, core), col: 8 (over z, y).
Axes of the slice: x: 2, y: 2, z: 4, core: 2. Of those that a mesh axis runs over, the one named last changes fastest.
Arguments:
- object_field: float32 [2, 2048, 4096], P(None, 'row', 'col'), may hold values from -5 to 5
- probe: float32 [2, 2, 256, 256], replicated, may hold values from -5 to 5
- amplitudes: float32 [256, 256, 256], P(('row', 'col')), may hold values from 0 to 2.5
- positions: int32 [256, 2], P(('row', 'col')), may hold values from 0 to 3840, as said below
- counts: int32 [32], P(('row', 'col')), may hold values from 1 to 8, as said below
Outputs:
- new_object: float32 [2, 2048, 4096], P(None, 'row', 'col')
- new_probe: float32 [2, 2, 256, 256], replicated
Inputs may be any that keep to these rules, and one draw needn't show every extreme that they name: `positions`: each slot's patch lies inside the object, and its top-left pixel lies in the tile of the device that holds the slot. `counts`: one device holds exactly 8 live slots in every draw; the others fewer.
All inputs are finite; a program needn't handle non-finite values.
Results may differ from a plain program's by a relative error of at most 0.0003.
Values sent between devices are 32-bit elements; how exact they have to be, the bound alone decides.
No kernel may reach another device: no remote copies, remote signals or barrier semaphores. Data moves between devices by JAX's collectives and lax.ppermute only.
A program may use at most 256 MiB of HBM per device.

v0:
```python
import functools
import math

import jax
import jax.numpy as jnp
import ml_dtypes
import numpy as np
from jax import lax
from jax.experimental import pallas as pl
from jax.experimental.pallas import tpu as pltpu
from jax.sharding import PartitionSpec as P

F32 = jnp.float32
BF16 = jnp.bfloat16
MIB = 1024 * 1024
LONG = pl.CostEstimate(flops=30_000_000_000, bytes_accessed=4_000_000, transcendentals=0)
SHORT = pl.CostEstimate(flops=0, bytes_accessed=1_000_000, transcendentals=0)
FLOOR = 0.3


def split_np(table):
    high = table.astype(ml_dtypes.bfloat16)
    low = (table - high.astype(np.float64)).astype(ml_dtypes.bfloat16)
    return high, low


def dft_tables(length):
    half = length // 2
    q = np.arange(half)[:, None]
    n = np.arange(half)[None, :]
    forward = []
    for odd in range(2):
        phase = (n * (2 * q + odd)) % length
        angle = phase * (-2.0 * math.pi / length)
        re = np.cos(angle) / math.sqrt(length)
        im = np.sin(angle) / math.sqrt(length)
        forward.append(np.stack(split_np(np.block([[re, -im], [im, re]]))))
    forward = np.stack(forward)
    return forward, np.ascontiguousarray(forward.transpose(0, 1, 3, 2))


def in_hbm(array):
    return pltpu.with_memory_space_constraint(array, pltpu.HBM)


def dot(a, b):
    return jnp.dot(a, b, preferred_element_type=F32)


def split(x):
    high = x.astype(BF16)
    return high, (x - high.astype(F32)).astype(BF16)


def roll_rows(x, shift):
    return pltpu.roll(x.reshape(x.shape[0] // 8, 8, x.shape[1]), shift, 1)


def roll_rows(x, shift):
    return pltpu.roll(x.reshape(x.shape[0] // 8, 8, x.shape[1]), shift, 1)


def roll_rows(x, shift):
    return pltpu.roll(x.reshape(x.shape[0] // 8, 8, x.shape[1]), shift, 1)


def roll_rows(x, shift):
    return pltpu.roll(x.reshape(x.shape[0] // 8, 8, x.shape[1]), shift, 1)


def split_three(x):
    high = x.astype(BF16)
    rest = x - high.astype(F32)
    middle = rest.astype(BF16)
    return high, middle, (rest - middle.astype(F32)).astype(BF16)


def add_shifted(template, grid, where_t, where_g, top, left, size):
    top_s = top & 7
    top_b = pl.multiple_of(top - top_s, 8)
    left_s = left & 127
    left_b = pl.multiple_of(left - left_s, 128)
    step = 24
    wrapped = lax.broadcasted_iota(jnp.int32, (step, 128), 1) < left_s
    wrapped_rows = lax.broadcasted_iota(jnp.int32, (step // 8, 8, 128), 1) < top_s
    zero = jnp.zeros((step, 128), F32)
    blocks = size // 128
    for at in range(0, size + 8, step):
        parts = []
        for j in range(blocks):
            x = roll_rows(template[where_t + (pl.ds(at, step + 8), pl.ds(128 * j, 128))], top_s)
            x = jnp.where(wrapped_rows, x[:-1], x[1:]).reshape(step, 128)
            parts.append(pltpu.roll(x, left_s, 1))
        for j in range(blocks + 1):
            before = parts[j - 1] if j > 0 else zero
            after = parts[j] if j < blocks else zero
            spot = where_g + (pl.ds(top_b + at, step), pl.ds(left_b + 128 * j, 128))
            grid[spot] += jnp.where(wrapped, before, after)


def take_shifted(field, where, top, left, at, step, size):
    top_s = top & 7
    top_b = pl.multiple_of(top - top_s, 8)
    left_s = left & 127
    left_b = pl.multiple_of(left - left_s, 128)
    back = (128 - left_s) & 127
    keep = lax.broadcasted_iota(jnp.int32, (step + 8, 128), 1) < 128 - left_s
    keep_rows = lax.broadcasted_iota(jnp.int32, (step // 8, 8, 128), 1) < 8 - top_s
    blocks = size // 128
    parts = [
        pltpu.roll(field[where + (pl.ds(top_b + at, step + 8), pl.ds(left_b + 128 * j, 128))], back, 1)
        for j in range(blocks + 1)
    ]
    pieces = []
    for j in range(blocks):
        x = roll_rows(jnp.where(keep, parts[j], parts[j + 1]), (8 - top_s) & 7)
        pieces.append(jnp.where(keep_rows, x[:-1], x[1:]).reshape(step, 128))
    return jnp.concatenate(pieces, axis=1)


def light_kernel(slots, origin, meta, probe_h, top, corner, inverse_light, probe, template, grid, notes, sems):
    size = probe.shape[2]
    tile_rows, tile_cols = inverse_light.shape
    rows = pl.ds(top.shape[1] - 8, 8)
    cols = pl.ds(0, 128)
    copies = [
        pltpu.make_async_copy(top.at[0, rows, cols], notes.at[0], sems.at[0]),
        pltpu.make_async_copy(corner.at[0, rows, cols], notes.at[1], sems.at[1]),
        pltpu.make_async_copy(top.at[1, rows, cols], notes.at[2], sems.at[2]),
    ]
    copy = pltpu.make_async_copy(probe_h, probe, sems.at[3])
    copy.start()
    for item in copies:
        item.start()
    template[0:8, :] = jnp.zeros((8, size), F32)
    template[8 + size :, :] = jnp.zeros((8, size), F32)
    copy.wait()
    for at in range(0, size, 32):
        rows = pl.ds(at, 32)
        total = jnp.zeros((32, size), F32)
        for m in range(probe.shape[0]):
            total += probe[m, 0, rows] * probe[m, 0, rows] + probe[m, 1, rows] * probe[m, 1, rows]
        template[pl.ds(8 + at, 32), :] = total

    @pl.loop(0, tile_rows // 32)
    def _(step):
        rows = pl.ds(pl.multiple_of(size + step * 32, 32), 32)
        grid[rows, size : size + tile_cols] = jnp.zeros((32, tile_cols), F32)

    def add(top, left):
        @pl.when((top > 0) & (left > 0))
        def _():
            add_shifted(template, grid, (), (), top, left, size)

    @pl.loop(0, meta[0, 2 * slots])
    def _(slot):
        add(meta[0, 2 * slot] + size, meta[0, 2 * slot + 1] + size)

    for item in copies:
        item.wait()
    for device in range(3):

        @pl.loop(0, notes[device, 0, 2 * slots].astype(jnp.int32))
        def _(slot):
            top = notes[device, 0, 2 * slot].astype(jnp.int32) - meta[0, origin]
            left = notes[device, 0, 2 * slot + 1].astype(jnp.int32) - meta[0, origin + 1]
            add(top + size, left + size)

    @pl.loop(0, tile_rows // 32)
    def _(step):
        rows = pl.ds(pl.multiple_of(size + step * 32, 32), 32)
        out_rows = pl.ds(pl.multiple_of(step * 32, 32), 32)
        inverse_light[out_rows, :] = 1.0 / (grid[rows, size : size + tile_cols] + 1.0)


def light(meta, slots, origin, probe, top, corner, tile_shape):
    size = probe.shape[2]
    hbm = pl.BlockSpec(memory_space=pltpu.HBM)
    anywhere = pl.BlockSpec(memory_space=pl.ANY)
    return pl.pallas_call(
        functools.partial(light_kernel, slots, origin),
        out_shape=jax.ShapeDtypeStruct(tile_shape, F32),
        in_specs=[pl.BlockSpec(memory_space=pltpu.SMEM), hbm, anywhere, anywhere],
        out_specs=pl.BlockSpec(memory_space=pltpu.VMEM),
        scratch_shapes=[
            pltpu.VMEM(probe.shape, F32),
            pltpu.VMEM((size + 16, size), F32),
            pltpu.VMEM((tile_shape[0] + 2 * size, tile_shape[1] + 2 * size), F32),
            pltpu.SMEM((3, 8, 128), F32),
            pltpu.SemaphoreType.DMA((4,)),
        ],
        compiler_params=pltpu.CompilerParams(vmem_limit_bytes=8 * MIB),
        cost_estimate=pl.CostEstimate(flops=4_000_000_000, bytes_accessed=1_000_000, transcendentals=0),
        name="light",
    )(meta, in_hbm(probe), top, corner)


def arrange_kernel(meta, amplitudes, out, given, moved, in_sems, out_sems):
    slots, size, _ = amplitudes.shape
    count = meta[0, 2 * slots]

    def load(slot):
        return pltpu.make_async_copy(amplitudes.at[slot], given.at[slot], in_sems.at[slot])

    def store(slot):
        return pltpu.make_async_copy(moved.at[slot], out.at[slot], out_sems.at[slot])

    @pl.loop(0, count)
    def _(slot):
        load(slot).start()

    first = lax.broadcasted_iota(jnp.int32, (size, size), 0)
    second = lax.broadcasted_iota(jnp.int32, (size, size), 1)
    half = size // 2

    def source(index):
        return jnp.where(index < half, 2 * index, 2 * index - (size - 1))

    rows = (source(first) == second).astype(F32).astype(BF16)
    cols = (source(second) == first).astype(F32).astype(BF16)
    rows = jnp.concatenate([rows, rows], axis=1)
    cols = jnp.concatenate([cols, cols], axis=0)

    @pl.loop(0, count)
    def _(slot):
        load(slot).wait()
        x = dot(rows, jnp.concatenate(split(given[slot]), axis=0))
        moved[slot] = dot(jnp.concatenate(split(x), axis=1), cols)
        store(slot).start()

    @pl.loop(0, count)
    def _(slot):
        store(slot).wait()


def arrange(meta, amplitudes):
    slots = amplitudes.shape[0]
    hbm = pl.BlockSpec(memory_space=pltpu.HBM)
    return pl.pallas_call(
        arrange_kernel,
        out_shape=pltpu.HBM(amplitudes.shape, F32),
        in_specs=[pl.BlockSpec(memory_space=pltpu.SMEM), hbm],
        out_specs=hbm,
        scratch_shapes=[
            pltpu.VMEM(amplitudes.shape, F32),
            pltpu.VMEM(amplitudes.shape, F32),
            pltpu.SemaphoreType.DMA((slots,)),
            pltpu.SemaphoreType.DMA((slots,)),
        ],
        compiler_params=pltpu.CompilerParams(vmem_limit_bytes=8 * MIB),
        cost_estimate=LONG,
        name="arrange",
    )(meta, in_hbm(amplitudes))


def three_left(table, t):
    return jnp.concatenate([table[t, 0], table[t, 0], table[t, 1]], axis=1)


def three_right(table, v):
    return jnp.concatenate([table[v, 0], table[v, 0], table[v, 1]], axis=0)


def weave(first, second):
    total = max(len(first), len(second))
    done = [0, 0]
    for i in range(1, total + 1):
        for k, pieces in enumerate((first, second)):
            while done[k] * total < i * len(pieces):
                pieces[done[k]]()
                done[k] += 1


def slots_kernel(
    needs_rim, meta, probe, amplitudes, sources, forward_h, backward_h, init, note, outs, probe_out,
    ext, grid, amp, forward_t, backward_t, chosen, patch_f, patch_b, x_f, y_f, z_f, g_s, x_b, z_b, back, template, sums, sems,
):
    size = probe.shape[2]
    half = size // 2
    modes = probe.shape[0]
    slots = amplitudes.shape[0]
    tile_rows, tile_cols = (n - size for n in ext.shape[1:])
    step = 32
    fine = 16
    load_sems, amp_sems, out_sems = sems
    sums_out = probe_out
    if not needs_rim:
        probe_out = sums

    regions = (
        (pl.ds(0, tile_rows), pl.ds(0, tile_cols)),
        (pl.ds(tile_rows, size), pl.ds(0, tile_cols)),
        (pl.ds(0, size), pl.ds(tile_cols, size)),
        (pl.ds(size, tile_rows - size), pl.ds(tile_cols, size)),
        (pl.ds(tile_rows, size), pl.ds(tile_cols, size)),
    )
    loads = [
        pltpu.make_async_copy(source, ext.at[:, rows, cols], load_sems.at[i])
        for i, (source, (rows, cols)) in enumerate(zip(sources, regions))
    ]
    loads.append(pltpu.make_async_copy(forward_h, forward_t, load_sems.at[7]))
    loads.append(pltpu.make_async_copy(backward_h, backward_t, load_sems.at[8]))
    late = []
    if needs_rim:
        late.append(pltpu.make_async_copy(init[1], probe_out, load_sems.at[6]))
        below = grid.at[:, pl.ds(tile_rows, size), pl.ds(0, tile_cols)]
        late.append(pltpu.make_async_copy(init[0], below, load_sems.at[5]))
    for load in loads + late:
        load.start()

    def amp_copy(slot):
        return pltpu.make_async_copy(amplitudes.at[slot], amp.at[slot], amp_sems.at[slot])

    def choose(slot, found):
        beyond = meta[0, 2 * slot + 1] + size > tile_cols
        wanted = beyond if needs_rim else jnp.logical_not(beyond)

        @pl.when(wanted)
        def _():
            chosen[found] = slot
            amp_copy(slot).start()

        return found + wanted.astype(jnp.int32)

    count = lax.fori_loop(0, meta[0, 2 * slots], choose, jnp.zeros((), jnp.int32))

    @pl.loop(0, tile_rows // step)
    def _(at):
        rows = pl.ds(pl.multiple_of(at * step, step), step)
        for c in range(2):
            grid[c, rows, :] = jnp.zeros((step, tile_cols + size), F32)

    @pl.loop(tile_rows // step, (tile_rows + size) // step)
    def _(at):
        rows = pl.ds(pl.multiple_of(at * step, step), step)
        for c in range(2):
            if needs_rim:
                grid[c, rows, tile_cols:] = jnp.zeros((step, size), F32)
            else:
                grid[c, rows, :] = jnp.zeros((step, tile_cols + size), F32)

    if not needs_rim:

        @pl.loop(0, size // step)
        def _(at):
            rows = pl.ds(pl.multiple_of(at * step, step), step)
            for c in range(2 * modes + 1):
                probe_out[c, rows, :] = jnp.zeros((step, size), F32)

    for c in range(2):
        template[c, 0:8, :] = jnp.zeros((8, size), F32)
        template[c, 8 + size :, :] = jnp.zeros((8, size), F32)
    for load in loads:
        load.wait()

    def corner(slot):
        return meta[0, 2 * slot], meta[0, 2 * slot + 1]

    def forward(slot):
        top, left = corner(slot)

        def take(at):
            for c in range(2):
                patch_f[c, pl.ds(at, step), :] = take_shifted(ext, (c,), top, left, at, step, size)

        def fold_rows(m, at):
            cols = pl.ds(m * size, size)
            parts = []
            for base in (at, half + at):
                rows = pl.ds(base, fine)
                pr, pi = patch_f[0, rows, :], patch_f[1, rows, :]
                qr, qi = probe[m, 0, rows, :], probe[m, 1, rows, :]
                parts.append((qr * pr - qi * pi, qr * pi + qi * pr))
            for c in range(2):
                rows = pl.ds(c * half + at, fine)
                for t, value in enumerate((parts[0][c] + parts[1][c], parts[0][c] - parts[1][c])):
                    x_f[t, 0, rows, cols], x_f[t, 1, rows, cols] = split(value)

        def dft_rows(m, t):
            cols = pl.ds(m * size, size)
            high = x_f[t, 0, :, cols]
            u = dot(three_left(forward_t, t), jnp.concatenate([high, x_f[t, 1, :, cols], high], axis=0))
            rows = pl.ds(m * size + t * half, half)
            for v, value in enumerate((u[:, :half] + u[:, half:], u[:, :half] - u[:, half:])):
                high, low = split(value)
                for c in range(2):
                    lanes = pl.ds(c * half, half)
                    y_f[v, 0, rows, lanes] = high[c * half : (c + 1) * half]
                    y_f[v, 1, rows, lanes] = low[c * half : (c + 1) * half]

        def dft_cols(v):
            high = y_f[v, 0]
            z_f[v] = dot(jnp.concatenate([high, y_f[v, 1], high], axis=1), three_right(backward_t, v))

        def scale(v, at):
            if v == 0 and at == 0:
                amp_copy(slot).wait()
            waves = [z_f[v, pl.ds(m * size + at, fine), :] for m in range(modes)]
            total = jnp.zeros((fine, half), F32)
            for wave in waves:
                total += wave[:, :half] * wave[:, :half] + wave[:, half:] * wave[:, half:]
            measured = amp[slot, pl.ds(at, fine), pl.ds(v * half, half)]
            factor = measured * lax.rsqrt(jnp.maximum(total, FLOOR * FLOOR)) - 1.0
            factor = jnp.concatenate([factor, factor], axis=1)
            for m in range(modes):
                rows = pl.ds(m * size + at, fine)
                g_s[v, 0, rows, :], g_s[v, 1, rows, :] = split(waves[m] * factor)

        pieces = [(take, at) for at in range(0, size, step)]
        for m in range(modes):
            pieces += [(fold_rows, m, at) for at in range(0, half, fine)]
            pieces += [(dft_rows, m, t) for t in range(2)]
        pieces += [(dft_cols, v) for v in range(2)]
        pieces += [(scale, v, at) for v in range(2) for at in range(0, size, fine)]
        return [functools.partial(*piece) for piece in pieces]

    def backward(slot):
        top, left = corner(slot)

        def dft_cols(v):
            high = g_s[v, 0]
            z_b[v] = dot(jnp.concatenate([high, g_s[v, 1], high], axis=1), three_right(forward_t, v))

        def unfold_cols(m, t, at):
            rows = pl.ds(m * size + t * half + at, step)
            even, odd = z_b[0, rows, :], z_b[1, rows, :]
            for v, value in enumerate((even + odd, even - odd)):
                high, low = split(value)
                cols = pl.ds(m * size + v * half, half)
                for c in range(2):
                    spot = pl.ds(c * half + at, step)
                    x_b[t, 0, spot, cols] = high[:, c * half : (c + 1) * half]
                    x_b[t, 1, spot, cols] = low[:, c * half : (c + 1) * half]

        def dft_rows(m, t):
            cols = pl.ds(m * size, size)
            high = x_b[t, 0, :, cols]
            back[m, t] = dot(three_left(backward_t, t), jnp.concatenate([high, x_b[t, 1, :, cols], high], axis=0))

        def gradients(at):
            waves = []
            for m in range(modes):
                pair = []
                for c in range(2):
                    rows = pl.ds(c * half + at, fine)
                    even, odd = back[m, 0, rows, :], back[m, 1, rows, :]
                    pair.append((even + odd, even - odd))
                waves.append(pair)
            for h in range(2):
                rows = pl.ds(h * half + at, fine)
                pr, pi = patch_b[0, rows, :], patch_b[1, rows, :]
                grad_r = jnp.zeros((fine, size), F32)
                grad_i = jnp.zeros((fine, size), F32)
                for m in range(modes):
                    br, bi = waves[m][0][h], waves[m][1][h]
                    qr, qi = probe[m, 0, rows, :], probe[m, 1, rows, :]
                    grad_r += qr * br + qi * bi
                    grad_i += qr * bi - qi * br
                    probe_out[2 * m, rows, :] += pr * br + pi * bi
                    probe_out[2 * m + 1, rows, :] += pr * bi - pi * br
                probe_out[2 * modes, rows, :] += pr * pr + pi * pi
                spot = pl.ds(8 + h * half + at, fine)
                template[0, spot, :] = grad_r
                template[1, spot, :] = grad_i

        def add(c):
            add_shifted(template, grid, (c,), (c,), top, left, size)

        pieces = [(dft_cols, v) for v in range(2)]
        for m in range(modes):
            pieces += [(unfold_cols, m, t, at) for t in range(2) for at in range(0, half, step)]
            pieces += [(dft_rows, m, t) for t in range(2)]
        pieces += [(gradients, at) for at in range(0, half, fine)]
        pieces += [(add, c) for c in range(2)]
        return [functools.partial(*piece) for piece in pieces]

    def hand_over():
        for at in range(0, size, step):
            for c in range(2):
                patch_b[c, pl.ds(at, step), :] = patch_f[c, pl.ds(at, step), :]

    @pl.when(count > 0)
    def _():
        weave(forward(chosen[0]), [])
        hand_over()
        for load in late:
            load.wait()

        def visit(index, _):
            weave(backward(chosen[index]), forward(chosen[index + 1]))
            hand_over()
            return 0

        lax.fori_loop(0, count - 1, visit, 0)
        weave(backward(chosen[count - 1]), [])

    @pl.when(count == 0)
    def _():
        for load in late:
            load.wait()

    if needs_rim:
        top, bottom, rest = pl.ds(0, size), pl.ds(size, tile_rows - size), pl.ds(tile_cols, size)
        note_rows = pl.ds(size, 8)
        parts = [
            grid.at[:, pl.ds(0, tile_rows), pl.ds(0, tile_cols)],
            grid.at[:, bottom, rest],
            grid.at[:, top, rest],
            grid.at[:, pl.ds(tile_rows, size), rest],
            grid.at[:, pl.ds(tile_rows, size), pl.ds(0, tile_cols)],
            note[0],
            note[0],
            probe_out.at[:, pl.ds(pl.multiple_of(meta[0, 2 * slots + 1] * half, half), half)],
        ]
        outs = [
            outs[0],
            outs[1],
            outs[2].at[:, top],
            outs[3].at[:, top],
            outs[4],
            outs[2].at[0, note_rows],
            outs[3].at[0, note_rows],
            outs[5],
        ]
    else:
        parts = [
            grid.at[:, pl.ds(0, tile_rows), pl.ds(0, tile_cols)],
            grid.at[:, pl.ds(tile_rows, size), pl.ds(0, tile_cols)],
            sums,
        ]
        outs = [*outs, sums_out]
    stores = [pltpu.make_async_copy(part, out, out_sems.at[i]) for i, (part, out) in enumerate(zip(parts, outs))]
    for store in stores:
        store.start()
    for store in stores:
        store.wait()


def visit_slots(meta, probe, amplitudes, sources, init, note=()):
    size = probe.shape[2]
    modes = probe.shape[0]
    slots = amplitudes.shape[0]
    rows, cols = sources[0].shape[1:]
    tables = [jnp.asarray(item) for item in dft_tables(size)]
    vmem = pl.BlockSpec(memory_space=pltpu.VMEM)
    anywhere = pl.BlockSpec(memory_space=pl.ANY)
    hbm = pl.BlockSpec(memory_space=pltpu.HBM)
    needs_rim = bool(init)
    if needs_rim:
        shapes = [
            (2, rows, cols),
            (2, rows - size, size),
            (2, size + 8, size),
            (2, size + 8, size),
            (2, size, cols),
            (2 * modes + 1, size // 2, size),
        ]
    else:
        shapes = [(2, rows, cols), (2, size, cols)]
    splits = np.cumsum([1, 1, 1, len(sources), 1, 1, len(init), len(note), len(shapes), 1])

    def kernel(*refs):
        meta, probe, amplitudes, sources, forward_t, backward_t, init, note, outs, probe_out = (
            refs[a:b] for a, b in zip([0, *splits[:-1]], splits)
        )
        scratch = refs[splits[-1] :]
        slots_kernel(
            needs_rim, meta[0], probe[0], amplitudes[0], sources, forward_t[0], backward_t[0], init, note, outs,
            probe_out[0], *scratch[:-3], scratch[-3:],
        )

    return pl.pallas_call(
        kernel,
        out_shape=[pltpu.HBM(shapes[0], F32)]
        + [(jax.ShapeDtypeStruct if needs_rim else pltpu.HBM)(shape, F32) for shape in shapes[1:]]
        + [(jax.ShapeDtypeStruct if needs_rim else pltpu.HBM)((2 * modes + 1, size, size), F32)],
        in_specs=[pl.BlockSpec(memory_space=pltpu.SMEM), vmem, hbm, hbm] + [anywhere] * (len(sources) - 1)
        + [hbm] * (2 + len(init)) + [anywhere] * len(note),
        out_specs=[hbm] + [anywhere if needs_rim else hbm] * (len(shapes) - 1) + [vmem if needs_rim else hbm],
        scratch_shapes=[
            pltpu.VMEM((2, rows + size, cols + size), F32),
            pltpu.VMEM((2, rows + size, cols + size), F32),
            pltpu.VMEM(amplitudes.shape, F32),
            pltpu.VMEM(tables[0].shape, BF16),
            pltpu.VMEM(tables[1].shape, BF16),
            pltpu.SMEM((slots,), jnp.int32),
            pltpu.VMEM((2, size, size), F32),
            pltpu.VMEM((2, size, size), F32),
            pltpu.VMEM((2, 2, size, modes * size), BF16),
            pltpu.VMEM((2, 2, modes * size, size), BF16),
            pltpu.VMEM((2, modes * size, size), F32),
            pltpu.VMEM((2, 2, modes * size, size), BF16),
            pltpu.VMEM((2, 2, size, modes * size), BF16),
            pltpu.VMEM((2, modes * size, size), F32),
            pltpu.VMEM((modes, 2, size, size), F32),
            pltpu.VMEM((2, size + 16, size), F32),
            pltpu.VMEM((8, 128) if needs_rim else (2 * modes + 1, size, size), F32),
            pltpu.SemaphoreType.DMA((9,)),
            pltpu.SemaphoreType.DMA((slots,)),
            pltpu.SemaphoreType.DMA((8,)),
        ],
        compiler_params=pltpu.CompilerParams(vmem_limit_bytes=26 * MIB),
        cost_estimate=pl.CostEstimate(flops=12_000_000_000, bytes_accessed=16_000_000, transcendentals=0),
        name="slots_beyond" if needs_rim else "slots_inside",
    )(
        meta, probe, *map(in_hbm, [amplitudes, sources[0]]), *sources[1:], *map(in_hbm, [*tables, *init]), *note
    )


def finish_kernel(
    own, first, top, bottom, lower, scale, tile, out, own_s, first_s, right_s, lower_s, scale_s, tile_s, in_sems, out_sems
):
    size = right_s.shape[2]
    block = 128
    blocks = own_s.shape[1] // block

    def copies(i):
        rows = pl.ds(i * block, block)
        pairs = [
            (own.at[:, rows], own_s.at[:, rows]),
            (first.at[:, rows], first_s.at[:, rows]),
            (scale.at[rows], scale_s.at[rows]),
            (tile.at[:, rows], tile_s.at[:, rows]),
        ]
        if i < size // block:
            pairs.append((top.at[:, rows], right_s.at[:, rows]))
            pairs.append((lower.at[:, rows], lower_s.at[:, rows]))
        else:
            pairs.append((bottom.at[:, pl.ds(i * block - size, block)], right_s.at[:, rows]))
        return [pltpu.make_async_copy(a, b, in_sems.at[i, k]) for k, (a, b) in enumerate(pairs)]

    loads = [copies(i) for i in range(blocks)]
    for load in loads:
        for copy in load:
            copy.start()
    stores = []
    for i in range(blocks):
        for copy in loads[i]:
            copy.wait()
        rows = pl.ds(i * block, block)
        for at in range(i * block, (i + 1) * block, 32):
            part = pl.ds(at, 32)
            for c in range(2):
                near = own_s[c, part, :size] + first_s[c, part, :size] + right_s[c, part, :]
                far = own_s[c, part, size:] + first_s[c, part, size:]
                if i < size // block:
                    near, far = near + lower_s[c, part, :size], far + lower_s[c, part, size:]
                own_s[c, part, :size] = tile_s[c, part, :size] + near * scale_s[part, :size]
                own_s[c, part, size:] = tile_s[c, part, size:] + far * scale_s[part, size:]
        stores.append(pltpu.make_async_copy(own_s.at[:, rows], out.at[:, rows], out_sems.at[i]))
        stores[-1].start()
    for store in stores:
        store.wait()


def finish(own, first, top, bottom, lower, inverse_light, tile):
    rows, cols = tile.shape[1:]
    size = top.shape[2]
    hbm = pl.BlockSpec(memory_space=pltpu.HBM)
    return pl.pallas_call(
        finish_kernel,
        out_shape=jax.ShapeDtypeStruct(tile.shape, F32),
        in_specs=[hbm] * 2 + [pl.BlockSpec(memory_space=pl.ANY)] * 4 + [hbm],
        out_specs=hbm,
        scratch_shapes=[
            pltpu.VMEM(tile.shape, F32),
            pltpu.VMEM(tile.shape, F32),
            pltpu.VMEM((2, rows, size), F32),
            pltpu.VMEM((2, size, cols), F32),
            pltpu.VMEM((rows, cols), F32),
            pltpu.VMEM(tile.shape, F32),
            pltpu.SemaphoreType.DMA((rows // 128, 6)),
            pltpu.SemaphoreType.DMA((rows // 128,)),
        ],
        compiler_params=pltpu.CompilerParams(vmem_limit_bytes=12 * MIB),
        cost_estimate=pl.CostEstimate(flops=3_000_000, bytes_accessed=12_000_000, transcendentals=0),
        name="finish",
    )(in_hbm(own), in_hbm(first), top, bottom, lower, inverse_light, in_hbm(tile))


def from_behind(array, axis, by):
    count = lax.axis_size(axis)
    pairs = [(i, i + by) for i in range(count) if 0 <= i + by < count]
    return lax.ppermute(array, axis, pairs)


def exchange(array, axis, bit):
    count = lax.axis_size(axis)
    return lax.ppermute(array, axis, [(i, i ^ bit) for i in range(count)])


def together(*arrays):
    return lax.optimization_barrier(arrays)


def cut(tile, regions, cost, name):
    def kernel(tile, *refs):
        sems = refs[-1]
        copies = [
            pltpu.make_async_copy(tile.at[:, pl.ds(at, height), pl.ds(0, width)], out, sems.at[i])
            for i, ((at, height, width), out) in enumerate(zip(regions, refs[:-1]))
        ]
        for copy in copies:
            copy.start()
        for copy in copies:
            copy.wait()

    return pl.pallas_call(
        kernel,
        out_shape=[jax.ShapeDtypeStruct((2, height, width), F32) for _, height, width in regions],
        in_specs=[pl.BlockSpec(memory_space=pltpu.HBM)],
        out_specs=[pl.BlockSpec(memory_space=pltpu.VMEM)] * len(regions),
        scratch_shapes=[pltpu.SemaphoreType.DMA((len(regions),))],
        compiler_params=pltpu.CompilerParams(vmem_limit_bytes=4 * MIB),
        cost_estimate=cost,
        name=name,
    )(in_hbm(tile))


def fold(places, index, mine, got, upper):
    count, half, width = got.shape
    quarter = half // 2

    def kernel(places, mine, got, send, keep):
        base = 0 if index is None else places[0, index] * half
        for k, out in ((1 - places[0, upper], send), (places[0, upper], keep)):
            for c in range(count):
                out[c] = (
                    mine[c, pl.ds(pl.multiple_of(base + k * quarter, quarter), quarter), :]
                    + got[c, pl.ds(pl.multiple_of(k * quarter, quarter), quarter), :]
                )

    vmem = pl.BlockSpec(memory_space=pltpu.VMEM)
    shape = jax.ShapeDtypeStruct((count, quarter, width), F32)
    return pl.pallas_call(
        kernel,
        out_shape=[shape, shape],
        in_specs=[pl.BlockSpec(memory_space=pltpu.SMEM), vmem, vmem],
        out_specs=[vmem, vmem],
        compiler_params=pltpu.CompilerParams(vmem_limit_bytes=6 * MIB),
        cost_estimate=SHORT,
        name="fold",
    )(places, mine, got)


def merge(right, corner):
    rows = right.shape[1] - 8

    def kernel(right, corner, out):
        for c in range(2):
            out[c, :rows, :] = right[c, :rows, :] + corner[c, :rows, :]
        out[0, rows:, :] = right[0, rows:, :]
        out[1, rows:, :] = corner[0, rows:, :]

    vmem = pl.BlockSpec(memory_space=pltpu.VMEM)
    return pl.pallas_call(
        kernel,
        out_shape=jax.ShapeDtypeStruct(right.shape, F32),
        in_specs=[vmem, vmem],
        out_specs=vmem,
        compiler_params=pltpu.CompilerParams(vmem_limit_bytes=4 * MIB),
        cost_estimate=SHORT,
        name="merge",
    )(right, corner)


def deal(places, me, terms, parts, rows):
    aligned = rows % 8 == 0
    if not aligned:
        count, _, width = terms[0].shape
        terms = [sum(terms).reshape(count, parts, rows, width).transpose(1, 0, 2, 3)]
    count, width = terms[0].shape[0 if aligned else 1], terms[0].shape[-1]

    def kernel(places, *refs):
        terms, outs = refs[:-parts], refs[-parts:]
        for k, out in enumerate(outs):
            j = places[0, me] ^ k
            for c in range(count):
                if aligned:
                    spot = pl.ds(pl.multiple_of(j * rows, rows), rows)
                    out[c] = sum(term[c, spot, :] for term in terms)
                else:
                    out[c] = terms[0][j, c]

    vmem = pl.BlockSpec(memory_space=pltpu.VMEM)
    return pl.pallas_call(
        kernel,
        out_shape=[jax.ShapeDtypeStruct((count, rows, width), F32)] * parts,
        in_specs=[pl.BlockSpec(memory_space=pltpu.SMEM)] + [vmem] * len(terms),
        out_specs=[vmem] * parts,
        compiler_params=pltpu.CompilerParams(vmem_limit_bytes=4 * MIB),
        cost_estimate=SHORT,
        name="deal",
    )(places, *terms)


def settle(places, start, probe, pieces):
    count, rows, width = pieces[0].shape
    if rows % 8:
        share = sum(pieces)
        old = lax.dynamic_slice_in_dim(probe, places[0, start], rows, axis=1)
        return old + share[:-1] / (share[-1:] + 1.0)

    def kernel(places, probe, *refs):
        pieces, (out, old, sem) = refs[:-3], refs[-3:]
        spot = pl.ds(pl.multiple_of(places[0, start], 8), rows)
        copy = pltpu.make_async_copy(probe.at[:, spot], old, sem.at[0])
        copy.start()
        share = sum(piece[...] for piece in pieces)
        copy.wait()
        out[...] = old[...] + share[:-1] / (share[-1:] + 1.0)

    vmem = pl.BlockSpec(memory_space=pltpu.VMEM)
    return pl.pallas_call(
        kernel,
        out_shape=jax.ShapeDtypeStruct((count - 1, rows, width), F32),
        in_specs=[pl.BlockSpec(memory_space=pltpu.SMEM), pl.BlockSpec(memory_space=pltpu.HBM)] + [vmem] * len(pieces),
        out_specs=vmem,
        scratch_shapes=[pltpu.VMEM((count - 1, rows, width), F32), pltpu.SemaphoreType.DMA((1,))],
        compiler_params=pltpu.CompilerParams(vmem_limit_bytes=4 * MIB),
        cost_estimate=SHORT,
        name="settle",
    )(places, in_hbm(probe), *pieces)


def collect(places, me, pieces):
    count, rows, width = pieces[0].shape
    parts = len(pieces)
    aligned = rows % 8 == 0
    shape = (count, parts * rows, width) if aligned else (parts, count, rows, width)

    def kernel(places, *refs):
        pieces, out = refs[:-1], refs[-1]
        for k, piece in enumerate(pieces):
            j = places[0, me] ^ k
            for c in range(count):
                if aligned:
                    out[c, pl.ds(pl.multiple_of(j * rows, rows), rows), :] = piece[c]
                else:
                    out[j, c] = piece[c]

    vmem = pl.BlockSpec(memory_space=pltpu.VMEM)
    out = pl.pallas_call(
        kernel,
        out_shape=jax.ShapeDtypeStruct(shape, F32),
        in_specs=[pl.BlockSpec(memory_space=pltpu.SMEM)] + [vmem] * parts,
        out_specs=vmem,
        compiler_params=pltpu.CompilerParams(vmem_limit_bytes=4 * MIB),
        cost_estimate=SHORT,
        name="collect",
    )(places, *pieces)
    if not aligned:
        out = out.transpose(1, 0, 2, 3).reshape(count, parts * rows, width)
    return out


def join(places, upper, mine, other):
    half = mine.shape[1]

    def kernel(places, mine, other, out, sems):
        copies = [
            pltpu.make_async_copy(source, out.at[:, pl.ds(pl.multiple_of(at * half, half), half)], sems.at[i])
            for i, (source, at) in enumerate(((mine, places[0, upper]), (other, 1 - places[0, upper])))
        ]
        for copy in copies:
            copy.start()
        for copy in copies:
            copy.wait()

    anywhere = pl.BlockSpec(memory_space=pl.ANY)
    return pl.pallas_call(
        kernel,
        out_shape=jax.ShapeDtypeStruct((mine.shape[0], 2 * half) + mine.shape[2:], F32),
        in_specs=[pl.BlockSpec(memory_space=pltpu.SMEM), anywhere, anywhere],
        out_specs=anywhere,
        scratch_shapes=[pltpu.SemaphoreType.DMA((2,))],
        compiler_params=pltpu.CompilerParams(vmem_limit_bytes=MIB),
        cost_estimate=pl.CostEstimate(flops=0, bytes_accessed=2_000_000, transcendentals=0),
        name="join",
    )(places, mine, other)


def body(object_field, probe, amplitudes, positions, counts):
    modes, _, size, _ = probe.shape
    tile_rows, tile_cols = object_field.shape[1:]
    slots = amplitudes.shape[0]
    origin = jnp.stack([lax.axis_index("row") * tile_rows, lax.axis_index("col") * tile_cols]).astype(jnp.int32)
    bits = [1 << k for k in range(lax.axis_size("row").bit_length() - 1)]
    uppers = [(lax.axis_index("row") & bit) // bit for bit in bits]

    def relative(table):
        return jnp.concatenate([table[:, : 2 * slots] - jnp.tile(origin, slots)[None], table[:, 2 * slots :]], axis=1)

    right_up, right_down = cut(
        object_field, ((0, size, size), (size, tile_rows - size, size)), SHORT, "cut_right"
    )
    right_up, right_down, after_right = together(right_up, right_down, object_field)
    right_up = from_behind(right_up, "col", -1)
    right_down = from_behind(right_down, "col", -1)
    (lower,) = cut(after_right, ((0, size, tile_cols),), LONG, "cut_lower")
    meta = jnp.concatenate([positions.reshape(1, 2 * slots), counts.reshape(1, 1)], axis=1)
    lower = from_behind(lower, "row", -1)

    parts = lax.axis_size("col")
    rows = (size >> len(bits)) // parts
    me = lax.axis_index("col")
    start = sum(upper * (size >> (k + 1)) for k, upper in enumerate(uppers)) + me * rows
    bit_at = 2 * slots + 2
    me_at = bit_at + len(bits)
    start_at, origin_at = me_at + 1, me_at + 2
    extra = [1 - uppers[0], *uppers, me, start, origin[0], origin[1]]
    mine = jnp.concatenate([relative(meta), jnp.stack([item.astype(jnp.int32) for item in extra])[None]], axis=1)
    note = jnp.pad(meta.astype(F32), ((0, 7), (0, size - meta.shape[1])))
    mine, note = together(mine, note)
    amplitudes = arrange(mine, amplitudes)
    right_up, amplitudes = together(right_up, amplitudes)
    corner = from_behind(right_up, "row", -1)
    amplitudes, lower = together(amplitudes, lower)
    init = visit_slots(mine, probe, amplitudes, [object_field, lower], [])
    right_up, right_down, corner, *init = together(right_up, right_down, corner, *init)
    own, bottom_spill, top_spill, corner_spill, lower_spill, send, share = visit_slots(
        mine, probe, amplitudes, [object_field, lower, right_up, right_down, corner], list(init[1:]), [note]
    )

    index = bit_at
    for k, bit in enumerate(bits):
        got = exchange(send, "row", bit)
        if k == 0:
            bottom_spill = from_behind(bottom_spill, "col", 1)
            corner_spill = from_behind(corner_spill, "row", 1)
        if k + 1 < len(bits):
            send, share = fold(mine, index, share, got, bit_at + k + 1)
            index = None
    got, bottom_spill, corner_spill, lower_spill = together(got, bottom_spill, corner_spill, lower_spill)
    lower_spill = from_behind(lower_spill, "row", 1)
    top_spill = from_behind(merge(top_spill, corner_spill), "col", 1)
    own_part, *pieces = deal(mine, me_at, [share, got], parts, rows)
    pieces = [exchange(piece, "col", k + 1) for k, piece in enumerate(pieces)]
    new = settle(mine, start_at, probe.reshape(2 * modes, size, size), [own_part, *pieces])
    new = collect(mine, me_at, [new] + [exchange(new, "col", k) for k in range(1, parts)])
    new, top_spill = together(new, top_spill)
    inverse_light = light(mine, slots, origin_at, probe, top_spill, corner_spill, (tile_rows, tile_cols))
    for k, bit in reversed(list(enumerate(bits))):
        if k == 0:
            new, own = together(new, own)
            new_object = finish(own, init[0], top_spill, bottom_spill, lower_spill, inverse_light, object_field)
        other = exchange(new, "row", bit)
        if k + 1 == len(bits):
            other, inverse_light = together(other, inverse_light)
        if k == 0:
            other, new_object = together(other, new_object)
        new = join(mine, bit_at + k, new, other)
    return (new_object, new.reshape(modes, 2, size, size))


def solution(mesh):
    in_specs = (
        P(None, "row", "col"),
        P(),
        P(("row", "col"), None, None),
        P(("row", "col"), None),
        P(("row", "col")),
    )
    out_specs = (P(None, "row", "col"), P())
    return jax.shard_map(body, mesh=mesh, in_specs=in_specs, out_specs=out_specs, check_vma=False)
```

profile of v0, /device:TPU:0, one launch (start us, length us, event | category | flops | bytes accessed | tf_op | source)
XLA Modules:
  0.0 140.3 jit_solution(14800010137816417643)
XLA Ops:
  0.6 2.2 %cut_right.1 = (f32[2,256,256]{2,1,0:T(8,128)}, f32[2,256,256]{2,1,0:T(8,128)}) custom-call(f32[2,512,512]{2,1,0:T(8,128)} %tile.11), custom_call_target="tpu_custom_call" | custom-call | bytes 1000000 | tf_op jit(solution)/shard_map/cut_right/pallas_call | solution.py:708
  2.9 1.3 collective-permute-start
  4.2 1.3 collective-permute-start.2
  5.5 1.2 cut_lower.1
  6.7 1.3 collective-permute-start.1
  9.3 4.3 %arrange.1.refs_2_ = f32[8,256,256]{2,1,0:T(8,128)} custom-call(s32[1,24]{1,0:T(1,128)S(1)} %pad_add_fusion.1.meta.refs_0_.places, f32[8,256,256]{2,1,0:T(8,128)} %amplitudes.1), custom_call_target="tpu_custom_call" | custom-call | flops 30000001024 | bytes 4000000 | tf_op jit(solution)/shard_map/arrange/pallas_call | solution.py:239
  13.5 7.2 %collective-permute-done.refs_5_ = f32[2,256,256]{2,1,0:T(8,128)S(1)} collective-permute-done((f32[2,256,256]{2,1,0:T(8,128)}, f32[2,256,256]{2,1,0:T(8,128)S(1)}, u32[]{:S(2)}, u32[]{:S(2)}) %collective-permute-start) | collective-permute-done | bytes 524320 | tf_op jit(solution)/shard_map/ppermute | solution.py:684
  20.7 1.3 collective-permute-start.3
  22.0 4.8 %slots_inside.1 = (f32[2,512,512]{2,1,0:T(8,128)}, f32[2,256,512]{2,1,0:T(8,128)}, f32[5,256,256]{2,1,0:T(8,128)}) custom-call(s32[1,24]{1,0:T(1,128)S(1)} %pad_add_fusion.1.meta.refs_0_.places, f32[2,2,256,256]{3,2,1,0:T(8,128)S(1)} %copy-done, f32[8,256,256]{2,1,0:T(8,128)} %arrange.1.refs_2_, f32[2,512,512]{2,1,0:T(8,128)} %tile.11, ...), custom_call_target="tpu_custom_call" | custom-call | flops 12000000000 | bytes 16000000 | tf_op jit(solution)/shard_map/slots_inside/pallas_call | solution.py:572
  26.8 4.3 %collective-permute-done.2.refs_6_ = f32[2,256,256]{2,1,0:T(8,128)S(1)} collective-permute-done((f32[2,256,256]{2,1,0:T(8,128)}, f32[2,256,256]{2,1,0:T(8,128)S(1)}, u32[]{:S(2)}, u32[]{:S(2)}) %collective-permute-start.2) | collective-permute-done | bytes 524320 | tf_op jit(solution)/shard_map/ppermute | solution.py:684
  31.1 17.1 %slots_beyond.1 = (f32[2,512,512]{2,1,0:T(8,128)}, f32[2,256,256]{2,1,0:T(8,128)S(1)}, f32[2,264,256]{2,1,0:T(8,128)S(1)}, f32[2,264,256]{2,1,0:T(8,128)S(1)}, f...) custom-call(s32[1,24]{1,0:T(1,128)S(1)} %pad_add_fusion.1.meta.refs_0_.places, ...), custom_call_target="tpu_custom_call" | custom-call | flops 12000000000 | bytes 16000000 | tf_op jit(solution)/shard_map/slots_beyond/pallas_call | solution.py:572
  48.3 2.4 %collective-permute-start.7 = (f32[2,264,256]{2,1,0:T(8,128)S(1)}, f32[2,264,256]{2,1,0:T(8,128)S(1)}, u32[]{:S(2)}, u32[]{:S(2)}) collective-permute-start(f32[2,264,256]{2,1,0:T(8,128)S(1)} %get-tuple-element.75), channel_id=1, source_target_pairs={{0,8},{8,16},{16,24},{1,9},{9,17},{17,25},{2,10},{10,18},{18,26},{... | collective-permute-start | bytes 1622024 | tf_op jit(solution)/shard_map/ppermute | solution.py:684
  50.7 1.3 collective-permute-start.6
  52.7 1.7 %collective-permute-start.5 = (f32[5,64,256]{2,1,0:T(8,128)S(1)}, f32[5,64,256]{2,1,0:T(8,128)S(1)}, u32[]{:S(2)}, u32[]{:S(2)}) collective-permute-start(f32[5,64,256]{2,1,0:T(8,128)S(1)} %get-tuple-element.73), channel_id=1, source_target_pairs={{0,16},{8,24},{16,0},{24,8},{1,17},{9,25},{17,1},{25,9},{2,18},{10... | collective-permute-start | bytes 983048 | tf_op jit(solution)/shard_map/ppermute | solution.py:689
  54.4 9.1 %collective-permute-done.6.bottom = f32[2,256,256]{2,1,0:T(8,128)S(1)} collective-permute-done((f32[2,256,256]{2,1,0:T(8,128)S(1)}, f32[2,256,256]{2,1,0:T(8,128)S(1)}, u32[]{:S(2)}, u32[]{:S(2)}) %collective-permute-start.6) | collective-permute-done | bytes 524320 | tf_op jit(solution)/shard_map/ppermute | solution.py:684
  63.7 18.9 %collective-permute-start.22 = (f32[2,264,256]{2,1,0:T(8,128)S(1)}, f32[2,264,256]{2,1,0:T(8,128)S(1)}, u32[]{:S(2)}, u32[]{:S(2)}) collective-permute-start(f32[2,264,256]{2,1,0:T(8,128)S(1)} %merge.1), channel_id=1, source_target_pairs={{0,1},{1,2},{2,3},{3,4},{4,5},{5,6},{6,7},{8,9},{9,10},{10,11},{11... | collective-permute-start | bytes 1622024 | tf_op jit(solution)/shard_map/ppermute | solution.py:684
  83.2 3.4 %collective-permute-start.8 = (f32[5,8,256]{2,1,0:T(8,128)S(1)}, f32[5,8,256]{2,1,0:T(8,128)S(1)}, u32[]{:S(2)}, u32[]{:S(2)}) collective-permute-start(f32[5,8,256]{2,1,0:T(8,128)S(1)} %get-tuple-element.79), channel_id=1, source_target_pairs={{0,1},{1,0},{2,3},{3,2},{4,5},{5,4},{6,7},{7,6},{8,9},{9,8},{10,11... | collective-permute-start | bytes 122888 | tf_op jit(solution)/shard_map/ppermute | solution.py:689
  86.6 1.5 %collective-permute-start.10 = (f32[5,8,256]{2,1,0:T(8,128)S(1)}, f32[5,8,256]{2,1,0:T(8,128)S(1)}, u32[]{:S(2)}, u32[]{:S(2)}) collective-permute-start(f32[5,8,256]{2,1,0:T(8,128)S(1)} %get-tuple-element.81), channel_id=1, source_target_pairs={{0,3},{1,2},{2,1},{3,0},{4,7},{5,6},{6,5},{7,4},{8,11},{9,10},{10,... | collective-permute-start | bytes 122888 | tf_op jit(solution)/shard_map/ppermute | solution.py:689
  88.2 7.0 %collective-permute-done.8.refs_1_ = f32[5,8,256]{2,1,0:T(8,128)S(1)} collective-permute-done((f32[5,8,256]{2,1,0:T(8,128)S(1)}, f32[5,8,256]{2,1,0:T(8,128)S(1)}, u32[]{:S(2)}, u32[]{:S(2)}) %collective-permute-start.8) | collective-permute-done | bytes 40992 | tf_op jit(solution)/shard_map/ppermute | solution.py:689
  95.1 1.3 collective-permute-start.25
  96.6 6.5 %collective-permute-start.13 = (f32[5,8,256]{2,1,0:T(8,128)S(1)}, f32[5,8,256]{2,1,0:T(8,128)S(1)}, u32[]{:S(2)}, u32[]{:S(2)}) collective-permute-start(f32[5,8,256]{2,1,0:T(8,128)S(1)} %get-tuple-element.84), channel_id=1, source_target_pairs={{0,6},{1,7},{2,4},{3,5},{4,2},{5,3},{6,0},{7,1},{8,14},{9,15},{10,... | collective-permute-start | bytes 122888 | tf_op jit(solution)/shard_map/ppermute | solution.py:689
  103.8 1.8 %collective-permute-done.13.refs_6_ = f32[5,8,256]{2,1,0:T(8,128)S(1)} collective-permute-done((f32[5,8,256]{2,1,0:T(8,128)S(1)}, f32[5,8,256]{2,1,0:T(8,128)S(1)}, u32[]{:S(2)}, u32[]{:S(2)}) %collective-permute-start.13) | collective-permute-done | bytes 40992 | tf_op jit(solution)/shard_map/ppermute | solution.py:689
  105.6 4.2 %collective-permute-done.14.refs_7_ = f32[5,8,256]{2,1,0:T(8,128)S(1)} collective-permute-done((f32[5,8,256]{2,1,0:T(8,128)S(1)}, f32[5,8,256]{2,1,0:T(8,128)S(1)}, u32[]{:S(2)}, u32[]{:S(2)}) %collective-permute-start.14) | collective-permute-done | bytes 40992 | tf_op jit(solution)/shard_map/ppermute | solution.py:689
  109.8 1.3 settle.1.refs_0_
  111.9 3.8 %collective-permute-start.20 = (f32[4,8,256]{2,1,0:T(8,128)S(1)}, f32[4,8,256]{2,1,0:T(8,128)S(1)}, u32[]{:S(2)}, u32[]{:S(2)}) collective-permute-start(f32[4,8,256]{2,1,0:T(8,128)S(1)} %settle.1.refs_0_), channel_id=1, source_target_pairs={{0,6},{1,7},{2,4},{3,5},{4,2},{5,3},{6,0},{7,1},{8,14},{9,15},{10,... | collective-permute-start | bytes 98312 | tf_op jit(solution)/shard_map/ppermute | solution.py:689
  115.7 2.2 %collective-permute-done.21.refs_7_ = f32[4,8,256]{2,1,0:T(8,128)S(1)} collective-permute-done((f32[4,8,256]{2,1,0:T(8,128)S(1)}, f32[4,8,256]{2,1,0:T(8,128)S(1)}, u32[]{:S(2)}, u32[]{:S(2)}) %collective-permute-start.21) | collective-permute-done | bytes 32800 | tf_op jit(solution)/shard_map/ppermute | solution.py:689
  119.4 2.3 %collective-permute-done.19.refs_5_ = f32[4,8,256]{2,1,0:T(8,128)S(1)} collective-permute-done((f32[4,8,256]{2,1,0:T(8,128)S(1)}, f32[4,8,256]{2,1,0:T(8,128)S(1)}, u32[]{:S(2)}, u32[]{:S(2)}) %collective-permute-start.19) | collective-permute-done | bytes 32800 | tf_op jit(solution)/shard_map/ppermute | solution.py:689
  123.8 1.8 %collective-permute-done.16.refs_2_ = f32[4,8,256]{2,1,0:T(8,128)S(1)} collective-permute-done((f32[4,8,256]{2,1,0:T(8,128)S(1)}, f32[4,8,256]{2,1,0:T(8,128)S(1)}, u32[]{:S(2)}, u32[]{:S(2)}) %collective-permute-start.16) | collective-permute-done | bytes 32800 | tf_op jit(solution)/shard_map/ppermute | solution.py:689
  127.2 3.2 %light.1.scale = f32[512,512]{1,0:T(8,128)S(1)} custom-call(s32[1,24]{1,0:T(1,128)S(1)} %pad_add_fusion.1.meta.refs_0_.places, f32[2,2,256,256]{3,2,1,0:T(8,128)} %probe_h.1, f32[2,264,256]{2,1,0:T(8,128)S(1)} %collective-permute-done.22.top, f32[2,264,256]{2,1,0:T(8,128)S(1)} %collective-permute-done.7.corner), custom_call_target="tpu_custom_call" | custom-call | flops 4000000000 | bytes 1000000 | tf_op jit(solution)/shard_map/light/pallas_call | solution.py:180
  130.4 3.2 %collective-permute-done.23.other = f32[4,64,256]{2,1,0:T(8,128)S(1)} collective-permute-done((f32[4,64,256]{2,1,0:T(8,128)S(1)}, f32[4,64,256]{2,1,0:T(8,128)S(1)}, u32[]{:S(2)}, u32[]{:S(2)}) %collective-permute-start.23) | collective-permute-done | bytes 262176 | tf_op jit(solution)/shard_map/ppermute | solution.py:689
  134.3 4.3 %finish.1 = f32[2,512,512]{2,1,0:T(8,128)} custom-call(f32[2,512,512]{2,1,0:T(8,128)} %get-tuple-element.93.own, f32[2,512,512]{2,1,0:T(8,128)} %get-tuple-element.94.first, f32[2,264,256]{2,1,0:T(8,128)S(1)} %collective-permute-done.22.top, f32[2,256,256]{2,1,0:T(8,128)S(1)} %collective-permute-done.6.bottom, ...), custom_call_target="tpu_custom_call" | custom-call | flops 3000000 | bytes 12000000 | tf_op jit(solution)/shard_map/finish/pallas_call | solution.py:660
  138.6 1.5 %join.3 = f32[4,256,256]{2,1,0:T(8,128)} custom-call(s32[1,24]{1,0:T(1,128)S(1)} %pad_add_fusion.1.meta.refs_0_.places, f32[4,128,256]{2,1,0:T(8,128)S(1)} %join.2.mine, f32[4,128,256]{2,1,0:T(8,128)S(1)} %collective-permute-done.24.other), custom_call_target="tpu_custom_call" | custom-call | bytes 2000000 | tf_op jit(solution)/shard_map/join/pallas_call | solution.py:871
  (48 shorter events, 9.4 us)
Async XLA Ops:
  2.8 6.0 %copy-start.1 = (s32[8,2]{0,1:T(2,128)S(1)}, s32[8,2]{0,1:T(2,128)}, u32[]{:S(2)}) copy-start(s32[8,2]{0,1:T(2,128)} %param.12) | copy-start | bytes 196
  2.9 17.8 %collective-permute-start = (f32[2,256,256]{2,1,0:T(8,128)}, f32[2,256,256]{2,1,0:T(8,128)S(1)}, u32[]{:S(2)}, u32[]{:S(2)}) collective-permute-start(f32[2,256,256]{2,1,0:T(8,128)} %get-tuple-element.54), channel_id=1, source_target_pairs={{1,0},{2,1},{3,2},{4,3},{5,4},{6,5},{7,6},{9,8},{10,9},{11,10},{12... | collective-permute-start | bytes 1572872 | tf_op jit(solution)/shard_map/ppermute | solution.py:684
  4.2 26.9 %collective-permute-start.2 = (f32[2,256,256]{2,1,0:T(8,128)}, f32[2,256,256]{2,1,0:T(8,128)S(1)}, u32[]{:S(2)}, u32[]{:S(2)}) collective-permute-start(f32[2,256,256]{2,1,0:T(8,128)} %get-tuple-element.60), channel_id=1, source_target_pairs={{1,0},{2,1},{3,2},{4,3},{5,4},{6,5},{7,6},{9,8},{10,9},{11,10},{12... | collective-permute-start | bytes 1572872 | tf_op jit(solution)/shard_map/ppermute | solution.py:684
  6.7 15.3 %collective-permute-start.1 = (f32[2,256,512]{2,1,0:T(8,128)S(1)}, f32[2,256,512]{2,1,0:T(8,128)S(1)}, u32[]{:S(2)}, u32[]{:S(2)}) collective-permute-start(f32[2,256,512]{2,1,0:T(8,128)S(1)} %cut_lower.1), channel_id=1, source_target_pairs={{8,0},{16,8},{24,16},{9,1},{17,9},{25,17},{10,2},{18,10},{26,18},{... | collective-permute-start | bytes 3145736 | tf_op jit(solution)/shard_map/ppermute | solution.py:684
  9.3 12.7 %copy-start = (f32[2,2,256,256]{3,2,1,0:T(8,128)S(1)}, f32[2,2,256,256]{3,2,1,0:T(8,128)}, u32[]{:S(2)}) copy-start(f32[2,2,256,256]{3,2,1,0:T(8,128)} %probe_h.1) | copy-start | bytes 3145732
  20.7 10.4 %collective-permute-start.3 = (f32[2,256,256]{2,1,0:T(8,128)S(1)}, f32[2,256,256]{2,1,0:T(8,128)S(1)}, u32[]{:S(2)}, u32[]{:S(2)}) collective-permute-start(f32[2,256,256]{2,1,0:T(8,128)S(1)} %collective-permute-done.refs_5_), channel_id=1, source_target_pairs={{8,0},{16,8},{24,16},{9,1},{17,9},{25,17},{10,2},{18,10},{26,18},{... | collective-permute-start | bytes 1572872 | tf_op jit(solution)/shard_map/ppermute | solution.py:684
  48.2 3.8 %collective-permute-start.4 = (f32[5,128,256]{2,1,0:T(8,128)S(1)}, f32[5,128,256]{2,1,0:T(8,128)S(1)}, u32[]{:S(2)}, u32[]{:S(2)}) collective-permute-start(f32[5,128,256]{2,1,0:T(8,128)S(1)} %get-tuple-element.71), channel_id=1, source_target_pairs={{0,8},{8,0},{16,24},{24,16},{1,9},{9,1},{17,25},{25,17},{2,10},{10... | collective-permute-start | bytes 1966088 | tf_op jit(solution)/shard_map/ppermute | solution.py:689
  48.3 15.3 %collective-permute-start.7 = (f32[2,264,256]{2,1,0:T(8,128)S(1)}, f32[2,264,256]{2,1,0:T(8,128)S(1)}, u32[]{:S(2)}, u32[]{:S(2)}) collective-permute-start(f32[2,264,256]{2,1,0:T(8,128)S(1)} %get-tuple-element.75), channel_id=1, source_target_pairs={{0,8},{8,16},{16,24},{1,9},{9,17},{17,25},{2,10},{10,18},{18,26},{... | collective-permute-start | bytes 1622024 | tf_op jit(solution)/shard_map/ppermute | solution.py:684
  50.7 12.8 %collective-permute-start.6 = (f32[2,256,256]{2,1,0:T(8,128)S(1)}, f32[2,256,256]{2,1,0:T(8,128)S(1)}, u32[]{:S(2)}, u32[]{:S(2)}) collective-permute-start(f32[2,256,256]{2,1,0:T(8,128)S(1)} %get-tuple-element.74), channel_id=1, source_target_pairs={{0,1},{1,2},{2,3},{3,4},{4,5},{5,6},{6,7},{8,9},{9,10},{10,11},{11... | collective-permute-start | bytes 1572872 | tf_op jit(solution)/shard_map/ppermute | solution.py:684
  52.7 10.9 %collective-permute-start.5 = (f32[5,64,256]{2,1,0:T(8,128)S(1)}, f32[5,64,256]{2,1,0:T(8,128)S(1)}, u32[]{:S(2)}, u32[]{:S(2)}) collective-permute-start(f32[5,64,256]{2,1,0:T(8,128)S(1)} %get-tuple-element.73), channel_id=1, source_target_pairs={{0,16},{8,24},{16,0},{24,8},{1,17},{9,25},{17,1},{25,9},{2,18},{10... | collective-permute-start | bytes 983048 | tf_op jit(solution)/shard_map/ppermute | solution.py:689
  63.7 63.5 %collective-permute-start.22 = (f32[2,264,256]{2,1,0:T(8,128)S(1)}, f32[2,264,256]{2,1,0:T(8,128)S(1)}, u32[]{:S(2)}, u32[]{:S(2)}) collective-permute-start(f32[2,264,256]{2,1,0:T(8,128)S(1)} %merge.1), channel_id=1, source_target_pairs={{0,1},{1,2},{2,3},{3,4},{4,5},{5,6},{6,7},{8,9},{9,10},{10,11},{11... | collective-permute-start | bytes 1622024 | tf_op jit(solution)/shard_map/ppermute | solution.py:684
  83.2 11.9 %collective-permute-start.8 = (f32[5,8,256]{2,1,0:T(8,128)S(1)}, f32[5,8,256]{2,1,0:T(8,128)S(1)}, u32[]{:S(2)}, u32[]{:S(2)}) collective-permute-start(f32[5,8,256]{2,1,0:T(8,128)S(1)} %get-tuple-element.79), channel_id=1, source_target_pairs={{0,1},{1,0},{2,3},{3,2},{4,5},{5,4},{6,7},{7,6},{8,9},{9,8},{10,11... | collective-permute-start | bytes 122888 | tf_op jit(solution)/shard_map/ppermute | solution.py:689
  86.6 9.9 %collective-permute-start.9 = (f32[5,8,256]{2,1,0:T(8,128)S(1)}, f32[5,8,256]{2,1,0:T(8,128)S(1)}, u32[]{:S(2)}, u32[]{:S(2)}) collective-permute-start(f32[5,8,256]{2,1,0:T(8,128)S(1)} %get-tuple-element.80), channel_id=1, source_target_pairs={{0,2},{1,3},{2,0},{3,1},{4,6},{5,7},{6,4},{7,5},{8,10},{9,11},{10,... | collective-permute-start | bytes 122888 | tf_op jit(solution)/shard_map/ppermute | solution.py:689
  86.6 10.0 %collective-permute-start.10 = (f32[5,8,256]{2,1,0:T(8,128)S(1)}, f32[5,8,256]{2,1,0:T(8,128)S(1)}, u32[]{:S(2)}, u32[]{:S(2)}) collective-permute-start(f32[5,8,256]{2,1,0:T(8,128)S(1)} %get-tuple-element.81), channel_id=1, source_target_pairs={{0,3},{1,2},{2,1},{3,0},{4,7},{5,6},{6,5},{7,4},{8,11},{9,10},{10,... | collective-permute-start | bytes 122888 | tf_op jit(solution)/shard_map/ppermute | solution.py:689
  88.2 14.9 %collective-permute-start.11 = (f32[5,8,256]{2,1,0:T(8,128)S(1)}, f32[5,8,256]{2,1,0:T(8,128)S(1)}, u32[]{:S(2)}, u32[]{:S(2)}) collective-permute-start(f32[5,8,256]{2,1,0:T(8,128)S(1)} %get-tuple-element.82), channel_id=1, source_target_pairs={{0,4},{1,5},{2,6},{3,7},{4,0},{5,1},{6,2},{7,3},{8,12},{9,13},{10,... | collective-permute-start | bytes 122888 | tf_op jit(solution)/shard_map/ppermute | solution.py:689
  95.1 39.1 %collective-permute-start.25 = (f32[2,256,512]{2,1,0:T(8,128)S(1)}, f32[2,256,512]{2,1,0:T(8,128)S(1)}, u32[]{:S(2)}, u32[]{:S(2)}) collective-permute-start(f32[2,256,512]{2,1,0:T(8,128)S(1)} %get-tuple-element.96), channel_id=1, source_target_pairs={{0,8},{8,16},{16,24},{1,9},{9,17},{17,25},{2,10},{10,18},{18,26},{... | collective-permute-start | bytes 3145736 | tf_op jit(solution)/shard_map/ppermute | solution.py:684
  96.5 7.3 %collective-permute-start.12 = (f32[5,8,256]{2,1,0:T(8,128)S(1)}, f32[5,8,256]{2,1,0:T(8,128)S(1)}, u32[]{:S(2)}, u32[]{:S(2)}) collective-permute-start(f32[5,8,256]{2,1,0:T(8,128)S(1)} %get-tuple-element.83), channel_id=1, source_target_pairs={{0,5},{1,4},{2,7},{3,6},{4,1},{5,0},{6,3},{7,2},{8,13},{9,12},{10,... | collective-permute-start | bytes 122888 | tf_op jit(solution)/shard_map/ppermute | solution.py:689
  96.6 9.0 %collective-permute-start.13 = (f32[5,8,256]{2,1,0:T(8,128)S(1)}, f32[5,8,256]{2,1,0:T(8,128)S(1)}, u32[]{:S(2)}, u32[]{:S(2)}) collective-permute-start(f32[5,8,256]{2,1,0:T(8,128)S(1)} %get-tuple-element.84), channel_id=1, source_target_pairs={{0,6},{1,7},{2,4},{3,5},{4,2},{5,3},{6,0},{7,1},{8,14},{9,15},{10,... | collective-permute-start | bytes 122888 | tf_op jit(solution)/shard_map/ppermute | solution.py:689
  103.1 6.7 %collective-permute-start.14 = (f32[5,8,256]{2,1,0:T(8,128)S(1)}, f32[5,8,256]{2,1,0:T(8,128)S(1)}, u32[]{:S(2)}, u32[]{:S(2)}) collective-permute-start(f32[5,8,256]{2,1,0:T(8,128)S(1)} %get-tuple-element.85), channel_id=1, source_target_pairs={{0,7},{1,6},{2,5},{3,4},{4,3},{5,2},{6,1},{7,0},{8,15},{9,14},{10,... | collective-permute-start | bytes 122888 | tf_op jit(solution)/shard_map/ppermute | solution.py:689
  111.1 6.7 %collective-permute-start.21 = (f32[4,8,256]{2,1,0:T(8,128)S(1)}, f32[4,8,256]{2,1,0:T(8,128)S(1)}, u32[]{:S(2)}, u32[]{:S(2)}) collective-permute-start(f32[4,8,256]{2,1,0:T(8,128)S(1)} %settle.1.refs_0_), channel_id=1, source_target_pairs={{0,7},{1,6},{2,5},{3,4},{4,3},{5,2},{6,1},{7,0},{8,15},{9,14},{10,... | collective-permute-start | bytes 98312 | tf_op jit(solution)/shard_map/ppermute | solution.py:689
  111.9 6.9 %collective-permute-start.20 = (f32[4,8,256]{2,1,0:T(8,128)S(1)}, f32[4,8,256]{2,1,0:T(8,128)S(1)}, u32[]{:S(2)}, u32[]{:S(2)}) collective-permute-start(f32[4,8,256]{2,1,0:T(8,128)S(1)} %settle.1.refs_0_), channel_id=1, source_target_pairs={{0,6},{1,7},{2,4},{3,5},{4,2},{5,3},{6,0},{7,1},{8,14},{9,15},{10,... | collective-permute-start | bytes 98312 | tf_op jit(solution)/shard_map/ppermute | solution.py:689
  115.7 6.1 %collective-permute-start.19 = (f32[4,8,256]{2,1,0:T(8,128)S(1)}, f32[4,8,256]{2,1,0:T(8,128)S(1)}, u32[]{:S(2)}, u32[]{:S(2)}) collective-permute-start(f32[4,8,256]{2,1,0:T(8,128)S(1)} %settle.1.refs_0_), channel_id=1, source_target_pairs={{0,5},{1,4},{2,7},{3,6},{4,1},{5,0},{6,3},{7,2},{8,13},{9,12},{10,... | collective-permute-start | bytes 98312 | tf_op jit(solution)/shard_map/ppermute | solution.py:689
  117.8 4.8 %collective-permute-start.18 = (f32[4,8,256]{2,1,0:T(8,128)S(1)}, f32[4,8,256]{2,1,0:T(8,128)S(1)}, u32[]{:S(2)}, u32[]{:S(2)}) collective-permute-start(f32[4,8,256]{2,1,0:T(8,128)S(1)} %settle.1.refs_0_), channel_id=1, source_target_pairs={{0,4},{1,5},{2,6},{3,7},{4,0},{5,1},{6,2},{7,3},{8,12},{9,13},{10,... | collective-permute-start | bytes 98312 | tf_op jit(solution)/shard_map/ppermute | solution.py:689
  118.8 5.0 %collective-permute-start.17 = (f32[4,8,256]{2,1,0:T(8,128)S(1)}, f32[4,8,256]{2,1,0:T(8,128)S(1)}, u32[]{:S(2)}, u32[]{:S(2)}) collective-permute-start(f32[4,8,256]{2,1,0:T(8,128)S(1)} %settle.1.refs_0_), channel_id=1, source_target_pairs={{0,3},{1,2},{2,1},{3,0},{4,7},{5,6},{6,5},{7,4},{8,11},{9,10},{10,... | collective-permute-start | bytes 98312 | tf_op jit(solution)/shard_map/ppermute | solution.py:689
  121.7 3.9 %collective-permute-start.16 = (f32[4,8,256]{2,1,0:T(8,128)S(1)}, f32[4,8,256]{2,1,0:T(8,128)S(1)}, u32[]{:S(2)}, u32[]{:S(2)}) collective-permute-start(f32[4,8,256]{2,1,0:T(8,128)S(1)} %settle.1.refs_0_), channel_id=1, source_target_pairs={{0,2},{1,3},{2,0},{3,1},{4,6},{5,7},{6,4},{7,5},{8,10},{9,11},{10,... | collective-permute-start | bytes 98312 | tf_op jit(solution)/shard_map/ppermute | solution.py:689
  122.6 3.9 %collective-permute-start.15 = (f32[4,8,256]{2,1,0:T(8,128)S(1)}, f32[4,8,256]{2,1,0:T(8,128)S(1)}, u32[]{:S(2)}, u32[]{:S(2)}) collective-permute-start(f32[4,8,256]{2,1,0:T(8,128)S(1)} %settle.1.refs_0_), channel_id=1, source_target_pairs={{0,1},{1,0},{2,3},{3,2},{4,5},{5,4},{6,7},{7,6},{8,9},{9,8},{10,11... | collective-permute-start | bytes 98312 | tf_op jit(solution)/shard_map/ppermute | solution.py:689
  127.1 6.4 %collective-permute-start.23 = (f32[4,64,256]{2,1,0:T(8,128)S(1)}, f32[4,64,256]{2,1,0:T(8,128)S(1)}, u32[]{:S(2)}, u32[]{:S(2)}) collective-permute-start(f32[4,64,256]{2,1,0:T(8,128)S(1)} %collect.1.mine), channel_id=1, source_target_pairs={{0,16},{8,24},{16,0},{24,8},{1,17},{9,25},{17,1},{25,9},{2,18},{10... | collective-permute-start | bytes 786440 | tf_op jit(solution)/shard_map/ppermute | solution.py:689
  134.2 4.4 %collective-permute-start.24 = (f32[4,128,256]{2,1,0:T(8,128)S(1)}, f32[4,128,256]{2,1,0:T(8,128)S(1)}, u32[]{:S(2)}, u32[]{:S(2)}) collective-permute-start(f32[4,128,256]{2,1,0:T(8,128)S(1)} %join.2.mine), channel_id=1, source_target_pairs={{0,8},{8,0},{16,24},{24,16},{1,9},{9,1},{17,25},{25,17},{2,10},{10... | collective-permute-start | bytes 1572872 | tf_op jit(solution)/shard_map/ppermute | solution.py:689
where the time goes:
time: 138 us; the launch traced here: 140 us
  starting transfers between devices  50.7 us (37%)
  waiting for transfers between devices  44.9 us (33%)
  Pallas kernels  42.4 us (31%)
  between operations  1.73 us (1%)
    ppermute x8, starting transfers between devices, from_behind(): return lax.ppermute(array, axis, pairs)  29.2 us
    ppermute x18, waiting for transfers between devices, exchange(): return lax.ppermute(array, axis, [(i, i ^ bit) for i in range(count)])  24.3 us
    pallas_call x2, Pallas kernels, visit_slots(): pl.pallas_call(kernel, out_shape=[pltpu.HBM(shapes[0], F32)] + [(jax.Shap...  21.9 us
    ppermute x18, starting transfers between devices, exchange(): return lax.ppermute(array, axis, [(i, i ^ bit) for i in range(count)])  21.5 us
    ppermute x8, waiting for transfers between devices, from_behind(): return lax.ppermute(array, axis, pairs)  20.6 us
    pallas_call x1, Pallas kernels, finish(): pl.pallas_call(finish_kernel, out_shape=jax.ShapeDtypeStruct(tile.shape,...  4.34 us
    pallas_call x1, Pallas kernels, arrange(): pl.pallas_call(arrange_kernel, out_shape=pltpu.HBM(amplitudes.shape, F32)...  4.25 us
    pallas_call x2, Pallas kernels, cut(): pl.pallas_call(kernel, out_shape=[jax.ShapeDtypeStruct((2, height, width)...  3.45 us
  transfers between devices with their start and end apart: 26, of which 12 were waited for; matrix products, arithmetic and copies ran while one was open for 0% of the time, Pallas kernels for 15%

commit v1 on v0

--- a/solution.py
+++ b/solution.py
@@ -125,7 +125,7 @@
     cols = pl.ds(0, 128)
     copies = [
         pltpu.make_async_copy(top.at[0, rows, cols], notes.at[0], sems.at[0]),
-        pltpu.make_async_copy(corner.at[0, rows, cols], notes.at[1], sems.at[1]),
+        pltpu.make_async_copy(corner.at[0, pl.ds(corner.shape[1] - 8, 8), cols], notes.at[1], sems.at[1]),
         pltpu.make_async_copy(top.at[1, rows, cols], notes.at[2], sems.at[2]),
     ]
     copy = pltpu.make_async_copy(probe_h, probe, sems.at[3])
@@ -272,9 +272,10 @@
 
 
 def slots_kernel(
-    needs_rim, meta, probe, amplitudes, sources, forward_h, backward_h, init, note, outs, probe_out,
-    ext, grid, amp, forward_t, backward_t, chosen, patch_f, patch_b, x_f, y_f, z_f, g_s, x_b, z_b, back, template, sums, sems,
+    needs_rim, meta, probe, amplitudes, sources, tables, note, state, outs,
+    amp, chosen, patch_f, patch_b, x_f, y_f, z_f, g_s, x_b, z_b, back, template, load_sems, amp_sems, out_sems,
 ):
+    ext, grid, probe_out, forward_t, backward_t = state
     size = probe.shape[2]
     half = size // 2
     modes = probe.shape[0]
@@ -282,30 +283,22 @@
     tile_rows, tile_cols = (n - size for n in ext.shape[1:])
     step = 32
     fine = 16
-    load_sems, amp_sems, out_sems = sems
-    sums_out = probe_out
-    if not needs_rim:
-        probe_out = sums
-
-    regions = (
-        (pl.ds(0, tile_rows), pl.ds(0, tile_cols)),
-        (pl.ds(tile_rows, size), pl.ds(0, tile_cols)),
-        (pl.ds(0, size), pl.ds(tile_cols, size)),
-        (pl.ds(size, tile_rows - size), pl.ds(tile_cols, size)),
-        (pl.ds(tile_rows, size), pl.ds(tile_cols, size)),
-    )
+
+    body_rows, rim_rows = pl.ds(0, tile_rows), pl.ds(tile_rows, size)
+    body_cols, rim_cols = pl.ds(0, tile_cols), pl.ds(tile_cols, size)
+    if needs_rim:
+        places = [
+            ext.at[:, pl.ds(0, size), rim_cols],
+            ext.at[:, pl.ds(size, tile_rows - size), rim_cols],
+            ext.at[:, rim_rows, rim_cols],
+        ]
+    else:
+        places = [ext.at[:, body_rows, body_cols], ext.at[:, rim_rows, body_cols], forward_t, backward_t]
     loads = [
-        pltpu.make_async_copy(source, ext.at[:, rows, cols], load_sems.at[i])
-        for i, (source, (rows, cols)) in enumerate(zip(sources, regions))
+        pltpu.make_async_copy(source, place, load_sems.at[i])
+        for i, (source, place) in enumerate(zip([*sources, *tables], places))
     ]
-    loads.append(pltpu.make_async_copy(forward_h, forward_t, load_sems.at[7]))
-    loads.append(pltpu.make_async_copy(backward_h, backward_t, load_sems.at[8]))
-    late = []
-    if needs_rim:
-        late.append(pltpu.make_async_copy(init[1], probe_out, load_sems.at[6]))
-        below = grid.at[:, pl.ds(tile_rows, size), pl.ds(0, tile_cols)]
-        late.append(pltpu.make_async_copy(init[0], below, load_sems.at[5]))
-    for load in loads + late:
+    for load in loads:
         load.start()
 
     def amp_copy(slot):
@@ -324,22 +317,13 @@
 
     count = lax.fori_loop(0, meta[0, 2 * slots], choose, jnp.zeros((), jnp.int32))
 
-    @pl.loop(0, tile_rows // step)
-    def _(at):
-        rows = pl.ds(pl.multiple_of(at * step, step), step)
-        for c in range(2):
-            grid[c, rows, :] = jnp.zeros((step, tile_cols + size), F32)
-
-    @pl.loop(tile_rows // step, (tile_rows + size) // step)
-    def _(at):
-        rows = pl.ds(pl.multiple_of(at * step, step), step)
-        for c in range(2):
-            if needs_rim:
-                grid[c, rows, tile_cols:] = jnp.zeros((step, size), F32)
-            else:
+    if not needs_rim:
+
+        @pl.loop(0, (tile_rows + size) // step)
+        def _(at):
+            rows = pl.ds(pl.multiple_of(at * step, step), step)
+            for c in range(2):
                 grid[c, rows, :] = jnp.zeros((step, tile_cols + size), F32)
-
-    if not needs_rim:
 
         @pl.loop(0, size // step)
         def _(at):
@@ -483,8 +467,6 @@
     def _():
         weave(forward(chosen[0]), [])
         hand_over()
-        for load in late:
-            load.wait()
 
         def visit(index, _):
             weave(backward(chosen[index]), forward(chosen[index + 1]))
@@ -494,121 +476,105 @@
         lax.fori_loop(0, count - 1, visit, 0)
         weave(backward(chosen[count - 1]), [])
 
-    @pl.when(count == 0)
-    def _():
-        for load in late:
-            load.wait()
-
     if needs_rim:
-        top, bottom, rest = pl.ds(0, size), pl.ds(size, tile_rows - size), pl.ds(tile_cols, size)
         note_rows = pl.ds(size, 8)
         parts = [
-            grid.at[:, pl.ds(0, tile_rows), pl.ds(0, tile_cols)],
-            grid.at[:, bottom, rest],
-            grid.at[:, top, rest],
-            grid.at[:, pl.ds(tile_rows, size), rest],
-            grid.at[:, pl.ds(tile_rows, size), pl.ds(0, tile_cols)],
-            note[0],
-            note[0],
-            probe_out.at[:, pl.ds(pl.multiple_of(meta[0, 2 * slots + 1] * half, half), half)],
+            (grid.at[:, body_rows, body_cols], outs[0]),
+            (grid.at[:, body_rows, rim_cols], outs[1].at[:, body_rows]),
+            (note, outs[1].at[0, pl.ds(tile_rows, 8)]),
+            (grid.at[:, rim_rows, rim_cols], outs[2].at[:, pl.ds(0, size)]),
+            (note, outs[2].at[0, note_rows]),
+            (grid.at[:, rim_rows, body_cols], outs[3]),
+            (probe_out.at[:, pl.ds(pl.multiple_of(meta[0, 2 * slots + 1] * half, half), half)], outs[4]),
         ]
-        outs = [
-            outs[0],
-            outs[1],
-            outs[2].at[:, top],
-            outs[3].at[:, top],
-            outs[4],
-            outs[2].at[0, note_rows],
-            outs[3].at[0, note_rows],
-            outs[5],
-        ]
-    else:
-        parts = [
-            grid.at[:, pl.ds(0, tile_rows), pl.ds(0, tile_cols)],
-            grid.at[:, pl.ds(tile_rows, size), pl.ds(0, tile_cols)],
-            sums,
-        ]
-        outs = [*outs, sums_out]
-    stores = [pltpu.make_async_copy(part, out, out_sems.at[i]) for i, (part, out) in enumerate(zip(parts, outs))]
-    for store in stores:
-        store.start()
-    for store in stores:
-        store.wait()
-
-
-def visit_slots(meta, probe, amplitudes, sources, init, note=()):
-    size = probe.shape[2]
-    modes = probe.shape[0]
-    slots = amplitudes.shape[0]
-    rows, cols = sources[0].shape[1:]
+        stores = [pltpu.make_async_copy(part, out, out_sems.at[i]) for i, (part, out) in enumerate(parts)]
+        for store in stores:
+            store.start()
+        for store in stores:
+            store.wait()
+
+
+def scratch_for(size, modes, slots):
+    return [
+        pltpu.VMEM((slots, size, size), F32),
+        pltpu.SMEM((slots,), jnp.int32),
+        pltpu.VMEM((2, size, size), F32),
+        pltpu.VMEM((2, size, size), F32),
+        pltpu.VMEM((2, 2, size, modes * size), BF16),
+        pltpu.VMEM((2, 2, modes * size, size), BF16),
+        pltpu.VMEM((2, modes * size, size), F32),
+        pltpu.VMEM((2, 2, modes * size, size), BF16),
+        pltpu.VMEM((2, 2, size, modes * size), BF16),
+        pltpu.VMEM((2, modes * size, size), F32),
+        pltpu.VMEM((modes, 2, size, size), F32),
+        pltpu.VMEM((2, size + 16, size), F32),
+        pltpu.SemaphoreType.DMA((4,)),
+        pltpu.SemaphoreType.DMA((slots,)),
+        pltpu.SemaphoreType.DMA((7,)),
+    ]
+
+
+SLOTS_COST = pl.CostEstimate(flops=12_000_000_000, bytes_accessed=16_000_000, transcendentals=0)
+
+
+def visit_inside(meta, probe, amplitudes, tile, lower):
+    size, modes, slots = probe.shape[2], probe.shape[0], amplitudes.shape[0]
+    rows, cols = tile.shape[1:]
     tables = [jnp.asarray(item) for item in dft_tables(size)]
     vmem = pl.BlockSpec(memory_space=pltpu.VMEM)
+    hbm = pl.BlockSpec(memory_space=pltpu.HBM)
+    field = pltpu.VMEM((2, rows + size, cols + size), F32)
+
+    def kernel(meta, probe, amplitudes, tile, lower, forward_h, backward_h, *refs):
+        state, scratch = refs[:5], refs[5:]
+        slots_kernel(
+            False, meta, probe, amplitudes, [tile, lower], [forward_h, backward_h], None, state, None, *scratch
+        )
+
+    return pl.pallas_call(
+        kernel,
+        out_shape=[field, field, pltpu.VMEM((2 * modes + 1, size, size), F32)]
+        + [pltpu.VMEM(item.shape, BF16) for item in tables],
+        in_specs=[pl.BlockSpec(memory_space=pltpu.SMEM), vmem, hbm, hbm, pl.BlockSpec(memory_space=pl.ANY), hbm, hbm],
+        out_specs=[vmem] * 5,
+        scratch_shapes=scratch_for(size, modes, slots),
+        compiler_params=pltpu.CompilerParams(vmem_limit_bytes=28 * MIB),
+        cost_estimate=SLOTS_COST,
+        name="slots_inside",
+    )(meta, probe, in_hbm(amplitudes), in_hbm(tile), lower, *map(in_hbm, tables))
+
+
+def visit_beyond(meta, probe, amplitudes, rims, note, state):
+    size, modes, slots = probe.shape[2], probe.shape[0], amplitudes.shape[0]
+    rows, cols = (n - size for n in state[0].shape[1:])
+    vmem = pl.BlockSpec(memory_space=pltpu.VMEM)
+    hbm = pl.BlockSpec(memory_space=pltpu.HBM)
     anywhere = pl.BlockSpec(memory_space=pl.ANY)
-    hbm = pl.BlockSpec(memory_space=pltpu.HBM)
-    needs_rim = bool(init)
-    if needs_rim:
-        shapes = [
-            (2, rows, cols),
-            (2, rows - size, size),
-            (2, size + 8, size),
-            (2, size + 8, size),
-            (2, size, cols),
-            (2 * modes + 1, size // 2, size),
-        ]
-    else:
-        shapes = [(2, rows, cols), (2, size, cols)]
-    splits = np.cumsum([1, 1, 1, len(sources), 1, 1, len(init), len(note), len(shapes), 1])
-
-    def kernel(*refs):
-        meta, probe, amplitudes, sources, forward_t, backward_t, init, note, outs, probe_out = (
-            refs[a:b] for a, b in zip([0, *splits[:-1]], splits)
-        )
-        scratch = refs[splits[-1] :]
-        slots_kernel(
-            needs_rim, meta[0], probe[0], amplitudes[0], sources, forward_t[0], backward_t[0], init, note, outs,
-            probe_out[0], *scratch[:-3], scratch[-3:],
-        )
-
-    return pl.pallas_call(
+    shapes = [(2, rows + 8, size), (2, size + 8, size), (2, size, cols), (2 * modes + 1, size // 2, size)]
+
+    def kernel(meta, probe, amplitudes, *refs):
+        rims, note, refs = refs[:3], refs[3], refs[9:]
+        state, outs, scratch = refs[:5], refs[5:10], refs[10:]
+        slots_kernel(True, meta, probe, amplitudes, rims, [], note, state, outs, *scratch)
+
+    out = pl.pallas_call(
         kernel,
-        out_shape=[pltpu.HBM(shapes[0], F32)]
-        + [(jax.ShapeDtypeStruct if needs_rim else pltpu.HBM)(shape, F32) for shape in shapes[1:]]
-        + [(jax.ShapeDtypeStruct if needs_rim else pltpu.HBM)((2 * modes + 1, size, size), F32)],
-        in_specs=[pl.BlockSpec(memory_space=pltpu.SMEM), vmem, hbm, hbm] + [anywhere] * (len(sources) - 1)
-        + [hbm] * (2 + len(init)) + [anywhere] * len(note),
-        out_specs=[hbm] + [anywhere if needs_rim else hbm] * (len(shapes) - 1) + [vmem if needs_rim else hbm],
-        scratch_shapes=[
-            pltpu.VMEM((2, rows + size, cols + size), F32),
-            pltpu.VMEM((2, rows + size, cols + size), F32),
-            pltpu.VMEM(amplitudes.shape, F32),
-            pltpu.VMEM(tables[0].shape, BF16),
-            pltpu.VMEM(tables[1].shape, BF16),
-            pltpu.SMEM((slots,), jnp.int32),
-            pltpu.VMEM((2, size, size), F32),
-            pltpu.VMEM((2, size, size), F32),
-            pltpu.VMEM((2, 2, size, modes * size), BF16),
-            pltpu.VMEM((2, 2, modes * size, size), BF16),
-            pltpu.VMEM((2, modes * size, size), F32),
-            pltpu.VMEM((2, 2, modes * size, size), BF16),
-            pltpu.VMEM((2, 2, size, modes * size), BF16),
-            pltpu.VMEM((2, modes * size, size), F32),
-            pltpu.VMEM((modes, 2, size, size), F32),
-            pltpu.VMEM((2, size + 16, size), F32),
-            pltpu.VMEM((8, 128) if needs_rim else (2 * modes + 1, size, size), F32),
-            pltpu.SemaphoreType.DMA((9,)),
-            pltpu.SemaphoreType.DMA((slots,)),
-            pltpu.SemaphoreType.DMA((8,)),
-        ],
-        compiler_params=pltpu.CompilerParams(vmem_limit_bytes=26 * MIB),
-        cost_estimate=pl.CostEstimate(flops=12_000_000_000, bytes_accessed=16_000_000, transcendentals=0),
-        name="slots_beyond" if needs_rim else "slots_inside",
-    )(
-        meta, probe, *map(in_hbm, [amplitudes, sources[0]]), *sources[1:], *map(in_hbm, [*tables, *init]), *note
-    )
+        out_shape=[pltpu.VMEM(item.shape, item.dtype) for item in state]
+        + [pltpu.HBM((2, rows, cols), F32)]
+        + [jax.ShapeDtypeStruct(shape, F32) for shape in shapes],
+        in_specs=[pl.BlockSpec(memory_space=pltpu.SMEM), vmem, hbm] + [anywhere] * 4 + [vmem] * 5,
+        out_specs=[vmem] * 5 + [hbm] + [anywhere] * 4,
+        input_output_aliases={7 + i: i for i in range(5)},
+        scratch_shapes=scratch_for(size, modes, slots),
+        compiler_params=pltpu.CompilerParams(vmem_limit_bytes=28 * MIB),
+        cost_estimate=SLOTS_COST,
+        name="slots_beyond",
+    )(meta, probe, in_hbm(amplitudes), *rims, note, *state)
+    return (*out[5:], out[2])
 
 
 def finish_kernel(
-    own, first, top, bottom, lower, scale, tile, out, own_s, first_s, right_s, lower_s, scale_s, tile_s, in_sems, out_sems
+    own, right, lower, scale, tile, out, own_s, right_s, lower_s, scale_s, tile_s, in_sems, out_sems
 ):
     size = right_s.shape[2]
     block = 128
@@ -618,15 +584,12 @@
         rows = pl.ds(i * block, block)
         pairs = [
             (own.at[:, rows], own_s.at[:, rows]),
-            (first.at[:, rows], first_s.at[:, rows]),
+            (right.at[:, rows], right_s.at[:, rows]),
             (scale.at[rows], scale_s.at[rows]),
             (tile.at[:, rows], tile_s.at[:, rows]),
         ]
         if i < size // block:
-            pairs.append((top.at[:, rows], right_s.at[:, rows]))
             pairs.append((lower.at[:, rows], lower_s.at[:, rows]))
-        else:
-            pairs.append((bottom.at[:, pl.ds(i * block - size, block)], right_s.at[:, rows]))
         return [pltpu.make_async_copy(a, b, in_sems.at[i, k]) for k, (a, b) in enumerate(pairs)]
 
     loads = [copies(i) for i in range(blocks)]
@@ -641,8 +604,7 @@
         for at in range(i * block, (i + 1) * block, 32):
             part = pl.ds(at, 32)
             for c in range(2):
-                near = own_s[c, part, :size] + first_s[c, part, :size] + right_s[c, part, :]
-                far = own_s[c, part, size:] + first_s[c, part, size:]
+                near, far = own_s[c, part, :size] + right_s[c, part, :], own_s[c, part, size:]
                 if i < size // block:
                     near, far = near + lower_s[c, part, :size], far + lower_s[c, part, size:]
                 own_s[c, part, :size] = tile_s[c, part, :size] + near * scale_s[part, :size]
@@ -653,29 +615,28 @@
         store.wait()
 
 
-def finish(own, first, top, bottom, lower, inverse_light, tile):
+def finish(own, right, lower, inverse_light, tile):
     rows, cols = tile.shape[1:]
-    size = top.shape[2]
+    size = right.shape[2]
     hbm = pl.BlockSpec(memory_space=pltpu.HBM)
     return pl.pallas_call(
         finish_kernel,
         out_shape=jax.ShapeDtypeStruct(tile.shape, F32),
-        in_specs=[hbm] * 2 + [pl.BlockSpec(memory_space=pl.ANY)] * 4 + [hbm],
+        in_specs=[hbm] + [pl.BlockSpec(memory_space=pl.ANY)] * 3 + [hbm],
         out_specs=hbm,
         scratch_shapes=[
-            pltpu.VMEM(tile.shape, F32),
             pltpu.VMEM(tile.shape, F32),
             pltpu.VMEM((2, rows, size), F32),
             pltpu.VMEM((2, size, cols), F32),
             pltpu.VMEM((rows, cols), F32),
             pltpu.VMEM(tile.shape, F32),
-            pltpu.SemaphoreType.DMA((rows // 128, 6)),
+            pltpu.SemaphoreType.DMA((rows // 128, 5)),
             pltpu.SemaphoreType.DMA((rows // 128,)),
         ],
         compiler_params=pltpu.CompilerParams(vmem_limit_bytes=12 * MIB),
         cost_estimate=pl.CostEstimate(flops=3_000_000, bytes_accessed=12_000_000, transcendentals=0),
         name="finish",
-    )(in_hbm(own), in_hbm(first), top, bottom, lower, inverse_light, in_hbm(tile))
+    )(in_hbm(own), right, lower, inverse_light, in_hbm(tile))
 
 
 def from_behind(array, axis, by):
@@ -744,13 +705,14 @@
 
 
 def merge(right, corner):
-    rows = right.shape[1] - 8
+    rows, size = right.shape[1] - 8, right.shape[2]
 
     def kernel(right, corner, out):
         for c in range(2):
-            out[c, :rows, :] = right[c, :rows, :] + corner[c, :rows, :]
+            out[c, :size, :] = right[c, :size, :] + corner[c, :size, :]
+            out[c, size:rows, :] = right[c, size:rows, :]
         out[0, rows:, :] = right[0, rows:, :]
-        out[1, rows:, :] = corner[0, rows:, :]
+        out[1, rows:, :] = corner[0, size:, :]
 
     vmem = pl.BlockSpec(memory_space=pltpu.VMEM)
     return pl.pallas_call(
@@ -764,94 +726,80 @@
     )(right, corner)
 
 
-def deal(places, me, terms, parts, rows):
-    aligned = rows % 8 == 0
-    if not aligned:
-        count, _, width = terms[0].shape
-        terms = [sum(terms).reshape(count, parts, rows, width).transpose(1, 0, 2, 3)]
-    count, width = terms[0].shape[0 if aligned else 1], terms[0].shape[-1]
-
-    def kernel(places, *refs):
-        terms, outs = refs[:-parts], refs[-parts:]
-        for k, out in enumerate(outs):
-            j = places[0, me] ^ k
+def deal(terms, parts, rows):
+    count, _, width = terms[0].shape
+    if rows % 8:
+        return sum(terms).reshape(count, parts, rows, width).transpose(1, 0, 2, 3)
+
+    def kernel(*refs):
+        terms, out = refs[:-1], refs[-1]
+        for j in range(parts):
             for c in range(count):
-                if aligned:
-                    spot = pl.ds(pl.multiple_of(j * rows, rows), rows)
-                    out[c] = sum(term[c, spot, :] for term in terms)
-                else:
-                    out[c] = terms[0][j, c]
+                out[j, c] = sum(term[c, j * rows : (j + 1) * rows, :] for term in terms)
 
     vmem = pl.BlockSpec(memory_space=pltpu.VMEM)
     return pl.pallas_call(
         kernel,
-        out_shape=[jax.ShapeDtypeStruct((count, rows, width), F32)] * parts,
-        in_specs=[pl.BlockSpec(memory_space=pltpu.SMEM)] + [vmem] * len(terms),
-        out_specs=[vmem] * parts,
+        out_shape=jax.ShapeDtypeStruct((parts, count, rows, width), F32),
+        in_specs=[vmem] * len(terms),
+        out_specs=vmem,
         compiler_params=pltpu.CompilerParams(vmem_limit_bytes=4 * MIB),
         cost_estimate=SHORT,
         name="deal",
-    )(places, *terms)
+    )(*terms)
 
 
 def settle(places, start, probe, pieces):
-    count, rows, width = pieces[0].shape
+    parts, count, rows, width = pieces.shape
+    shape = (parts, count - 1, rows, width)
     if rows % 8:
-        share = sum(pieces)
+        share = pieces.sum(axis=0)
         old = lax.dynamic_slice_in_dim(probe, places[0, start], rows, axis=1)
-        return old + share[:-1] / (share[-1:] + 1.0)
-
-    def kernel(places, probe, *refs):
-        pieces, (out, old, sem) = refs[:-3], refs[-3:]
+        return jnp.broadcast_to((old + share[:-1] / (share[-1:] + 1.0))[None], shape)
+
+    def kernel(places, probe, pieces, out, old, sem):
         spot = pl.ds(pl.multiple_of(places[0, start], 8), rows)
         copy = pltpu.make_async_copy(probe.at[:, spot], old, sem.at[0])
         copy.start()
-        share = sum(piece[...] for piece in pieces)
+        share = sum(pieces[j] for j in range(parts))
         copy.wait()
-        out[...] = old[...] + share[:-1] / (share[-1:] + 1.0)
+        new = old[...] + share[:-1] / (share[-1:] + 1.0)
+        for j in range(parts):
+            out[j] = new
 
     vmem = pl.BlockSpec(memory_space=pltpu.VMEM)
     return pl.pallas_call(
         kernel,
-        out_shape=jax.ShapeDtypeStruct((count - 1, rows, width), F32),
-        in_specs=[pl.BlockSpec(memory_space=pltpu.SMEM), pl.BlockSpec(memory_space=pltpu.HBM)] + [vmem] * len(pieces),
+        out_shape=jax.ShapeDtypeStruct(shape, F32),
+        in_specs=[pl.BlockSpec(memory_space=pltpu.SMEM), pl.BlockSpec(memory_space=pltpu.HBM), vmem],
         out_specs=vmem,
-        scratch_shapes=[pltpu.VMEM((count - 1, rows, width), F32), pltpu.SemaphoreType.DMA((1,))],
+        scratch_shapes=[pltpu.VMEM(shape[1:], F32), pltpu.SemaphoreType.DMA((1,))],
         compiler_params=pltpu.CompilerParams(vmem_limit_bytes=4 * MIB),
         cost_estimate=SHORT,
         name="settle",
-    )(places, in_hbm(probe), *pieces)
-
-
-def collect(places, me, pieces):
-    count, rows, width = pieces[0].shape
-    parts = len(pieces)
-    aligned = rows % 8 == 0
-    shape = (count, parts * rows, width) if aligned else (parts, count, rows, width)
-
-    def kernel(places, *refs):
-        pieces, out = refs[:-1], refs[-1]
-        for k, piece in enumerate(pieces):
-            j = places[0, me] ^ k
+    )(places, in_hbm(probe), pieces)
+
+
+def collect(pieces):
+    parts, count, rows, width = pieces.shape
+    if rows % 8:
+        return pieces.transpose(1, 0, 2, 3).reshape(count, parts * rows, width)
+
+    def kernel(pieces, out):
+        for j in range(parts):
             for c in range(count):
-                if aligned:
-                    out[c, pl.ds(pl.multiple_of(j * rows, rows), rows), :] = piece[c]
-                else:
-                    out[j, c] = piece[c]
+                out[c, j * rows : (j + 1) * rows, :] = pieces[j, c]
 
     vmem = pl.BlockSpec(memory_space=pltpu.VMEM)
-    out = pl.pallas_call(
+    return pl.pallas_call(
         kernel,
-        out_shape=jax.ShapeDtypeStruct(shape, F32),
-        in_specs=[pl.BlockSpec(memory_space=pltpu.SMEM)] + [vmem] * parts,
+        out_shape=jax.ShapeDtypeStruct((count, parts * rows, width), F32),
+        in_specs=[vmem],
         out_specs=vmem,
         compiler_params=pltpu.CompilerParams(vmem_limit_bytes=4 * MIB),
         cost_estimate=SHORT,
         name="collect",
-    )(places, *pieces)
-    if not aligned:
-        out = out.transpose(1, 0, 2, 3).reshape(count, parts * rows, width)
-    return out
+    )(pieces)
 
 
 def join(places, upper, mine, other):
@@ -916,34 +864,32 @@
     right_up, amplitudes = together(right_up, amplitudes)
     corner = from_behind(right_up, "row", -1)
     amplitudes, lower = together(amplitudes, lower)
-    init = visit_slots(mine, probe, amplitudes, [object_field, lower], [])
-    right_up, right_down, corner, *init = together(right_up, right_down, corner, *init)
-    own, bottom_spill, top_spill, corner_spill, lower_spill, send, share = visit_slots(
-        mine, probe, amplitudes, [object_field, lower, right_up, right_down, corner], list(init[1:]), [note]
+    state = visit_inside(mine, probe, amplitudes, object_field, lower)
+    right_up, right_down, corner, *state = together(right_up, right_down, corner, *state)
+    own, right_spill, corner_spill, lower_spill, send, share = visit_beyond(
+        mine, probe, amplitudes, [right_up, right_down, corner], note, state
     )
 
     index = bit_at
     for k, bit in enumerate(bits):
         got = exchange(send, "row", bit)
         if k == 0:
-            bottom_spill = from_behind(bottom_spill, "col", 1)
             corner_spill = from_behind(corner_spill, "row", 1)
         if k + 1 < len(bits):
             send, share = fold(mine, index, share, got, bit_at + k + 1)
             index = None
-    got, bottom_spill, corner_spill, lower_spill = together(got, bottom_spill, corner_spill, lower_spill)
+    got, corner_spill, lower_spill = together(got, corner_spill, lower_spill)
     lower_spill = from_behind(lower_spill, "row", 1)
-    top_spill = from_behind(merge(top_spill, corner_spill), "col", 1)
-    own_part, *pieces = deal(mine, me_at, [share, got], parts, rows)
-    pieces = [exchange(piece, "col", k + 1) for k, piece in enumerate(pieces)]
-    new = settle(mine, start_at, probe.reshape(2 * modes, size, size), [own_part, *pieces])
-    new = collect(mine, me_at, [new] + [exchange(new, "col", k) for k in range(1, parts)])
-    new, top_spill = together(new, top_spill)
-    inverse_light = light(mine, slots, origin_at, probe, top_spill, corner_spill, (tile_rows, tile_cols))
+    right_spill = from_behind(merge(right_spill, corner_spill), "col", 1)
+    pieces = lax.all_to_all(deal([share, got], parts, rows), "col", 0, 0, tiled=True)
+    new = settle(mine, start_at, probe.reshape(2 * modes, size, size), pieces)
+    new = collect(lax.all_to_all(new, "col", 0, 0, tiled=True))
+    new, right_spill = together(new, right_spill)
+    inverse_light = light(mine, slots, origin_at, probe, right_spill, corner_spill, (tile_rows, tile_cols))
     for k, bit in reversed(list(enumerate(bits))):
         if k == 0:
             new, own = together(new, own)
-            new_object = finish(own, init[0], top_spill, bottom_spill, lower_spill, inverse_light, object_field)
+            new_object = finish(own, right_spill, lower_spill, inverse_light, object_field)
         other = exchange(new, "row", bit)
         if k + 1 == len(bits):
             other, inverse_light = together(other, inverse_light)

time: 138 us -> 136 us (0.986); the launches traced: 140 us -> 135 us
  blocking collectives: 0 us -> 24.1 us
  waiting for transfers between devices: 44.9 us -> 21.7 us
  Pallas kernels: 42.4 us -> 33.9 us
  starting transfers between devices: 50.7 us -> 52.1 us
    all_to_all x0 -> x1, blocking collectives: none -> 24.1 us  [body(): lax.all_to_all(deal([share, got], parts, rows), 'col', 0, 0, tiled=True)]
    ppermute x18 -> x4, waiting for transfers between devices: 24.3 us -> 10.9 us  [exchange(): return lax.ppermute(array, axis, [(i, i ^ bit) for i in range(count)])]
    ppermute x8 -> x7, waiting for transfers between devices: 20.6 us -> 7.67 us  [from_behind(): return lax.ppermute(array, axis, pairs)]
    ppermute x18 -> x4, starting transfers between devices: 21.5 us -> 13.4 us  [exchange(): return lax.ppermute(array, axis, [(i, i ^ bit) for i in range(count)])]
    all_to_all x0 -> x1, starting transfers between devices: none -> 7.94 us  [body(): new = collect(lax.all_to_all(new, 'col', 0, 0, tiled=True))]
    pallas_call x5, Pallas kernels: 24.3 us -> 17.5 us  [the longest x1 9.39 us: visit_inside(): pl.pallas_call(kernel, out_shape=[field, field, pltpu.VMEM((2 * modes + 1...]
    all_to_all x0 -> x1, waiting for transfers between devices: none -> 3.16 us  [body(): new = collect(lax.all_to_all(new, 'col', 0, 0, tiled=True))]
    ppermute x8 -> x7, starting transfers between devices: 29.2 us -> 30.8 us  [from_behind(): return lax.ppermute(array, axis, pairs)]
  transfers between devices with their start and end apart: 26 -> 12, of which waited for: 12 -> 4; matrix products, arithmetic and copies ran while one was open for 0% -> 0% of each run, Pallas kernels for 15% -> 18%
where the time goes in v1:
time: 136 us; the launch traced here: 135 us
  starting transfers between devices  52.1 us (38%)
  Pallas kernels  33.9 us (25%)
  blocking collectives  24.1 us (18%)
  waiting for transfers between devices  21.7 us (16%)
  between operations  1.67 us (1%)
  local copies, waits for them, and re-layouts  1.41 us (1%)
    ppermute x7, starting transfers between devices, from_behind(): return lax.ppermute(array, axis, pairs)  30.8 us
    all_to_all x1, blocking collectives, body(): lax.all_to_all(deal([share, got], parts, rows), 'col', 0, 0, tiled=True)  24.1 us
    ppermute x4, starting transfers between devices, exchange(): return lax.ppermute(array, axis, [(i, i ^ bit) for i in range(count)])  13.4 us
    ppermute x4, waiting for transfers between devices, exchange(): return lax.ppermute(array, axis, [(i, i ^ bit) for i in range(count)])  10.9 us
    pallas_call x1, Pallas kernels, visit_inside(): pl.pallas_call(kernel, out_shape=[field, field, pltpu.VMEM((2 * modes + 1...  9.39 us
    all_to_all x1, starting transfers between devices, body(): new = collect(lax.all_to_all(new, 'col', 0, 0, tiled=True))  7.94 us
    ppermute x7, waiting for transfers between devices, from_behind(): return lax.ppermute(array, axis, pairs)  7.67 us
    pallas_call x1, Pallas kernels, visit_beyond(): pl.pallas_call(kernel, out_shape=[pltpu.VMEM(item.shape, item.dtype) for...  6.05 us
  transfers between devices with their start and end apart: 12, of which 4 were waited for; matrix products, arithmetic and copies ran while one was open for 0% of the time, Pallas kernels for 18%

profile of v1, /device:TPU:0, one launch (start us, length us, event | category | flops | bytes accessed | tf_op | source)
XLA Modules:
  0.0 135.1 jit_solution(7731006523923476667)
XLA Ops:
  0.6 2.2 %cut_right.1 = (f32[2,256,256]{2,1,0:T(8,128)}, f32[2,256,256]{2,1,0:T(8,128)}) custom-call(f32[2,512,512]{2,1,0:T(8,128)} %tile.13), custom_call_target="tpu_custom_call" | custom-call | bytes 1000000 | tf_op jit(solution)/shard_map/cut_right/pallas_call | solution.py:669
  2.9 1.3 collective-permute-start
  4.2 1.3 collective-permute-start.2
  5.5 1.2 cut_lower.1
  6.7 1.3 collective-permute-start.1
  8.7 0.1 broadcast_in_dim_tile.3
  9.1 0.1 stack.35
  9.3 3.8 %arrange.1.amplitudes = f32[8,256,256]{2,1,0:T(8,128)} custom-call(s32[1,24]{1,0:T(1,128)S(1)} %pad_add_fusion.1.meta.places, f32[8,256,256]{2,1,0:T(8,128)} %amplitudes.1), custom_call_target="tpu_custom_call" | custom-call | flops 30000001024 | bytes 4000000 | tf_op jit(solution)/shard_map/arrange/pallas_call | solution.py:239
  13.0 7.7 %collective-permute-done.refs_0_ = f32[2,256,256]{2,1,0:T(8,128)S(1)} collective-permute-done((f32[2,256,256]{2,1,0:T(8,128)}, f32[2,256,256]{2,1,0:T(8,128)S(1)}, u32[]{:S(2)}, u32[]{:S(2)}) %collective-permute-start) | collective-permute-done | bytes 524320 | tf_op jit(solution)/shard_map/ppermute | solution.py:645
  20.7 1.3 collective-permute-start.3
  22.0 9.4 %slots_inside.1 = (f32[2,768,768]{2,1,0:T(8,128)S(1)}, f32[2,768,768]{2,1,0:T(8,128)S(1)}, f32[5,256,256]{2,1,0:T(8,128)S(1)}, bf16[2,2,256,256]{3,2,1,0:T(8,128)(2,1)S(1)}, bf16[2,2,256,256]{3,2,1,0:T(8,128)(2,1)S(1)}) custom-call(s32[1,24]{1,0:T(1,128)S(1)} %pad_add_fusion.1.meta.places, f32[2,2,256,256]{3,2,1,0:T(8,128)S(1)} %copy-done, ...), custom_call_target="tpu_custom_call" | custom-call | flops 12000000000 | bytes 16000000 | tf_op jit(solution)/shard_map/slots_inside/pallas_call | solution.py:534
  31.4 6.0 %slots_beyond.1 = (f32[2,768,768]{2,1,0:T(8,128)S(1)}, f32[2,768,768]{2,1,0:T(8,128)S(1)}, f32[5,256,256]{2,1,0:T(8,128)S(1)}, bf16[2,2,256,256]{3,2,1,0:T(8,128...) custom-call(s32[1,24]{1,0:T(1,128)S(1)} %pad_add_fusion.1.meta.place, ...), custom_call_target="tpu_custom_call", output_to_operand_aliasing={{0}: (7, {}), {1}: (8, {}), {2}: (9, {}), {3}: (10, {}), {4... | custom-call | flops 12000000000 | bytes 16000000 | tf_op jit(solution)/shard_map/slots_beyond/pallas_call | solution.py:560
  37.5 2.5 %collective-permute-start.4 = (f32[5,128,256]{2,1,0:T(8,128)S(1)}, f32[5,128,256]{2,1,0:T(8,128)S(1)}, u32[]{:S(2)}, u32[]{:S(2)}) collective-permute-start(f32[5,128,256]{2,1,0:T(8,128)S(1)} %get-tuple-element.70), channel_id=1, source_target_pairs={{0,8},{8,0},{16,24},{24,16},{1,9},{9,1},{17,25},{25,17},{2,10},{10... | collective-permute-start | bytes 1966088 | tf_op jit(solution)/shard_map/ppermute | solution.py:650
  40.0 2.0 %collective-permute-start.6 = (f32[2,264,256]{2,1,0:T(8,128)S(1)}, f32[2,264,256]{2,1,0:T(8,128)S(1)}, u32[]{:S(2)}, u32[]{:S(2)}) collective-permute-start(f32[2,264,256]{2,1,0:T(8,128)S(1)} %get-tuple-element.73), channel_id=1, source_target_pairs={{0,8},{8,16},{16,24},{1,9},{9,17},{17,25},{2,10},{10,18},{18,26},{... | collective-permute-start | bytes 1622024 | tf_op jit(solution)/shard_map/ppermute | solution.py:645
  41.9 0.6 fold.1
  42.6 2.7 %collective-permute-start.5 = (f32[5,64,256]{2,1,0:T(8,128)S(1)}, f32[5,64,256]{2,1,0:T(8,128)S(1)}, u32[]{:S(2)}, u32[]{:S(2)}) collective-permute-start(f32[5,64,256]{2,1,0:T(8,128)S(1)} %get-tuple-element.72), channel_id=1, source_target_pairs={{0,16},{8,24},{16,0},{24,8},{1,17},{9,25},{17,1},{25,9},{2,18},{10... | collective-permute-start | bytes 983048 | tf_op jit(solution)/shard_map/ppermute | solution.py:650
  45.2 8.2 %collective-permute-done.5.refs_1_ = f32[5,64,256]{2,1,0:T(8,128)S(1)} collective-permute-done((f32[5,64,256]{2,1,0:T(8,128)S(1)}, f32[5,64,256]{2,1,0:T(8,128)S(1)}, u32[]{:S(2)}, u32[]{:S(2)}) %collective-permute-start.5) | collective-permute-done | bytes 327712 | tf_op jit(solution)/shard_map/ppermute | solution.py:650
  53.4 0.1 merge.1
  53.5 18.6 %collective-permute-start.7 = (f32[2,520,256]{2,1,0:T(8,128)S(1)}, f32[2,520,256]{2,1,0:T(8,128)S(1)}, u32[]{:S(2)}, u32[]{:S(2)}) collective-permute-start(f32[2,520,256]{2,1,0:T(8,128)S(1)} %merge.1), channel_id=1, source_target_pairs={{0,1},{1,2},{2,3},{3,4},{4,5},{5,6},{6,7},{8,9},{9,10},{10,11},{11... | collective-permute-start | bytes 3194888 | tf_op jit(solution)/shard_map/ppermute | solution.py:645
  72.1 24.1 %all_to_all.10.pieces = f32[8,5,8,256]{3,2,1,0:T(8,128)S(1)} all-to-all(f32[8,5,8,256]{3,2,1,0:T(8,128)S(1)} %deal.1), channel_id=1, replica_groups=mesh['row'=4,'col'=8] {'col'}, dimensions={0} | all-to-all | bytes 655360 | tf_op jit(solution)/shard_map/all_to_all | solution.py:884
  96.3 2.0 %settle.1 = f32[8,4,8,256]{3,2,1,0:T(8,128)} custom-call(s32[1,24]{1,0:T(1,128)S(1)} %pad_add_fusion.1.meta.places, f32[4,256,256]{2,1,0:T(8,128)} %bitcast.13, f32[8,5,8,256]{3,2,1,0:T(8,128)S(1)} %all_to_all.10.pieces), custom_call_target="tpu_custom_call" | custom-call | bytes 1000000 | tf_op jit(solution)/shard_map/settle/pallas_call | solution.py:771
  98.3 7.9 %all-to-all-start.1 = ((f32[8,4,8,256]{3,2,1,0:T(8,128)}), f32[8,4,8,256]{3,2,1,0:T(8,128)S(1)}, u32[]{:S(2)}, u32[]{:S(2)}) async-start(f32[8,4,8,256]{3,2,1,0:T(8,128)} %settle.1), calls=%async_computation.1 | async-start | bytes 524288 | tf_op jit(solution)/shard_map/all_to_all | solution.py:886
  106.3 5.1 %collective-permute-start.10 = (f32[2,256,512]{2,1,0:T(8,128)}, f32[2,256,512]{2,1,0:T(8,128)S(1)}, u32[]{:S(2)}, u32[]{:S(2)}) collective-permute-start(f32[2,256,512]{2,1,0:T(8,128)} %copy-done.3), channel_id=1, source_target_pairs={{0,8},{8,16},{16,24},{1,9},{9,17},{17,25},{2,10},{10,18},{18,26},{... | collective-permute-start | bytes 3145736 | tf_op jit(solution)/shard_map/ppermute | solution.py:645
  111.4 3.2 %all-to-all-done.1.pieces = f32[8,4,8,256]{3,2,1,0:T(8,128)S(1)} async-done(((f32[8,4,8,256]{3,2,1,0:T(8,128)}), f32[8,4,8,256]{3,2,1,0:T(8,128)S(1)}, u32[]{:S(2)}, u32[]{:S(2)}) %all-to-all-start.1) | async-done | bytes 262176 | tf_op jit(solution)/shard_map/all_to_all | solution.py:886
  114.6 3.9 %collective-permute-start.8 = (f32[4,64,256]{2,1,0:T(8,128)S(1)}, f32[4,64,256]{2,1,0:T(8,128)S(1)}, u32[]{:S(2)}, u32[]{:S(2)}) collective-permute-start(f32[4,64,256]{2,1,0:T(8,128)S(1)} %collect.1.mine), channel_id=1, source_target_pairs={{0,16},{8,24},{16,0},{24,8},{1,17},{9,25},{17,1},{25,9},{2,18},{10... | collective-permute-start | bytes 786440 | tf_op jit(solution)/shard_map/ppermute | solution.py:650
  118.5 1.0 copy-done.2
  119.5 3.0 %light.1.scale = f32[512,512]{1,0:T(8,128)S(1)} custom-call(s32[1,24]{1,0:T(1,128)S(1)} %pad_add_fusion.1.meta.places, f32[2,2,256,256]{3,2,1,0:T(8,128)} %probe_h.1, f32[2,520,256]{2,1,0:T(8,128)S(1)} %collective-permute-done.7.top.right, f32[2,264,256]{2,1,0:T(8,128)S(1)} %copy-done.2), custom_call_target="tpu_custom_call" | custom-call | flops 4000000000 | bytes 1000000 | tf_op jit(solution)/shard_map/light/pallas_call | solution.py:180
  122.5 2.7 %collective-permute-done.8.other = f32[4,64,256]{2,1,0:T(8,128)S(1)} collective-permute-done((f32[4,64,256]{2,1,0:T(8,128)S(1)}, f32[4,64,256]{2,1,0:T(8,128)S(1)}, u32[]{:S(2)}, u32[]{:S(2)}) %collective-permute-start.8) | collective-permute-done | bytes 262176 | tf_op jit(solution)/shard_map/ppermute | solution.py:650
  125.2 0.6 join.2.mine
  125.8 4.3 %collective-permute-start.9 = (f32[4,128,256]{2,1,0:T(8,128)S(1)}, f32[4,128,256]{2,1,0:T(8,128)S(1)}, u32[]{:S(2)}, u32[]{:S(2)}) collective-permute-start(f32[4,128,256]{2,1,0:T(8,128)S(1)} %join.2.mine), channel_id=1, source_target_pairs={{0,8},{8,0},{16,24},{24,16},{1,9},{9,1},{17,25},{25,17},{2,10},{10... | collective-permute-start | bytes 1572872 | tf_op jit(solution)/shard_map/ppermute | solution.py:650
  130.2 3.3 %finish.1 = f32[2,512,512]{2,1,0:T(8,128)} custom-call(f32[2,512,512]{2,1,0:T(8,128)} %get-tuple-element.83.own, f32[2,520,256]{2,1,0:T(8,128)S(1)} %collective-permute-done.7.top.right, f32[2,256,512]{2,1,0:T(8,128)S(1)} %collective-permute-done.10.lower, f32[512,512]{1,0:T(8,128)S(1)} %light.1.scale, f32[2,512,512]{2,1,0:T(8,128)} %tile.13), custom_call_target="tpu_custom_call" | custom-call | flops 3000000 | bytes 12000000 | tf_op jit(solution)/shard_map/finish/pallas_call | solution.py:622
  133.4 1.5 %join.3 = f32[4,256,256]{2,1,0:T(8,128)} custom-call(s32[1,24]{1,0:T(1,128)S(1)} %pad_add_fusion.1.meta.places, f32[4,128,256]{2,1,0:T(8,128)S(1)} %join.2.mine, f32[4,128,256]{2,1,0:T(8,128)S(1)} %collective-permute-done.9.other), custom_call_target="tpu_custom_call" | custom-call | bytes 2000000 | tf_op jit(solution)/shard_map/join/pallas_call | solution.py:819
  (27 shorter events, 0.5 us)
Async XLA Ops:
  2.8 6.0 %copy-start.4 = (s32[8,2]{0,1:T(2,128)S(1)}, s32[8,2]{0,1:T(2,128)}, u32[]{:S(2)}) copy-start(s32[8,2]{0,1:T(2,128)} %param.10) | copy-start | bytes 196
  2.9 17.8 %collective-permute-start = (f32[2,256,256]{2,1,0:T(8,128)}, f32[2,256,256]{2,1,0:T(8,128)S(1)}, u32[]{:S(2)}, u32[]{:S(2)}) collective-permute-start(f32[2,256,256]{2,1,0:T(8,128)} %get-tuple-element.48), channel_id=1, source_target_pairs={{1,0},{2,1},{3,2},{4,3},{5,4},{6,5},{7,6},{9,8},{10,9},{11,10},{12... | collective-permute-start | bytes 1572872 | tf_op jit(solution)/shard_map/ppermute | solution.py:645
  4.2 27.2 %collective-permute-start.2 = (f32[2,256,256]{2,1,0:T(8,128)}, f32[2,256,256]{2,1,0:T(8,128)S(1)}, u32[]{:S(2)}, u32[]{:S(2)}) collective-permute-start(f32[2,256,256]{2,1,0:T(8,128)} %get-tuple-element.53), channel_id=1, source_target_pairs={{1,0},{2,1},{3,2},{4,3},{5,4},{6,5},{7,6},{9,8},{10,9},{11,10},{12... | collective-permute-start | bytes 1572872 | tf_op jit(solution)/shard_map/ppermute | solution.py:645
  6.7 15.3 %collective-permute-start.1 = (f32[2,256,512]{2,1,0:T(8,128)S(1)}, f32[2,256,512]{2,1,0:T(8,128)S(1)}, u32[]{:S(2)}, u32[]{:S(2)}) collective-permute-start(f32[2,256,512]{2,1,0:T(8,128)S(1)} %cut_lower.1), channel_id=1, source_target_pairs={{8,0},{16,8},{24,16},{9,1},{17,9},{25,17},{10,2},{18,10},{26,18},{... | collective-permute-start | bytes 3145736 | tf_op jit(solution)/shard_map/ppermute | solution.py:645
  9.3 12.7 %copy-start = (f32[2,2,256,256]{3,2,1,0:T(8,128)S(1)}, f32[2,2,256,256]{3,2,1,0:T(8,128)}, u32[]{:S(2)}) copy-start(f32[2,2,256,256]{3,2,1,0:T(8,128)} %probe_h.1) | copy-start | bytes 3145732
  20.7 10.7 %collective-permute-start.3 = (f32[2,256,256]{2,1,0:T(8,128)S(1)}, f32[2,256,256]{2,1,0:T(8,128)S(1)}, u32[]{:S(2)}, u32[]{:S(2)}) collective-permute-start(f32[2,256,256]{2,1,0:T(8,128)S(1)} %collective-permute-done.refs_0_), channel_id=1, source_target_pairs={{8,0},{16,8},{24,16},{9,1},{17,9},{25,17},{10,2},{18,10},{26,18},{... | collective-permute-start | bytes 1572872 | tf_op jit(solution)/shard_map/ppermute | solution.py:645
  37.5 58.8 %copy-start.3 = (f32[2,256,512]{2,1,0:T(8,128)}, f32[2,256,512]{2,1,0:T(8,128)S(1)}, u32[]{:S(2)}) copy-start(f32[2,256,512]{2,1,0:T(8,128)S(1)} %get-tuple-element.84) | copy-start | bytes 3145732
  37.5 4.4 %collective-permute-start.4 = (f32[5,128,256]{2,1,0:T(8,128)S(1)}, f32[5,128,256]{2,1,0:T(8,128)S(1)}, u32[]{:S(2)}, u32[]{:S(2)}) collective-permute-start(f32[5,128,256]{2,1,0:T(8,128)S(1)} %get-tuple-element.70), channel_id=1, source_target_pairs={{0,8},{8,0},{16,24},{24,16},{1,9},{9,1},{17,25},{25,17},{2,10},{10... | collective-permute-start | bytes 1966088 | tf_op jit(solution)/shard_map/ppermute | solution.py:650
  40.0 5.3 %collective-permute-start.6 = (f32[2,264,256]{2,1,0:T(8,128)S(1)}, f32[2,264,256]{2,1,0:T(8,128)S(1)}, u32[]{:S(2)}, u32[]{:S(2)}) collective-permute-start(f32[2,264,256]{2,1,0:T(8,128)S(1)} %get-tuple-element.73), channel_id=1, source_target_pairs={{0,8},{8,16},{16,24},{1,9},{9,17},{17,25},{2,10},{10,18},{18,26},{... | collective-permute-start | bytes 1622024 | tf_op jit(solution)/shard_map/ppermute | solution.py:645
  42.6 10.8 %collective-permute-start.5 = (f32[5,64,256]{2,1,0:T(8,128)S(1)}, f32[5,64,256]{2,1,0:T(8,128)S(1)}, u32[]{:S(2)}, u32[]{:S(2)}) collective-permute-start(f32[5,64,256]{2,1,0:T(8,128)S(1)} %get-tuple-element.72), channel_id=1, source_target_pairs={{0,16},{8,24},{16,0},{24,8},{1,17},{9,25},{17,1},{25,9},{2,18},{10... | collective-permute-start | bytes 983048 | tf_op jit(solution)/shard_map/ppermute | solution.py:650
  45.2 51.0 %copy-start.1 = (f32[2,264,256]{2,1,0:T(8,128)}, f32[2,264,256]{2,1,0:T(8,128)S(1)}, u32[]{:S(2)}) copy-start(f32[2,264,256]{2,1,0:T(8,128)S(1)} %collective-permute-done.6.corner) | copy-start | bytes 1622020
  53.5 61.0 %collective-permute-start.7 = (f32[2,520,256]{2,1,0:T(8,128)S(1)}, f32[2,520,256]{2,1,0:T(8,128)S(1)}, u32[]{:S(2)}, u32[]{:S(2)}) collective-permute-start(f32[2,520,256]{2,1,0:T(8,128)S(1)} %merge.1), channel_id=1, source_target_pairs={{0,1},{1,2},{2,3},{3,4},{4,5},{5,6},{6,7},{8,9},{9,10},{10,11},{11... | collective-permute-start | bytes 3194888 | tf_op jit(solution)/shard_map/ppermute | solution.py:645
  98.3 16.2 %all-to-all-start.1 = ((f32[8,4,8,256]{3,2,1,0:T(8,128)}), f32[8,4,8,256]{3,2,1,0:T(8,128)S(1)}, u32[]{:S(2)}, u32[]{:S(2)}) async-start(f32[8,4,8,256]{3,2,1,0:T(8,128)} %settle.1), calls=%async_computation.1 | async-start | bytes 524288 | tf_op jit(solution)/shard_map/all_to_all | solution.py:886
  106.3 23.9 %collective-permute-start.10 = (f32[2,256,512]{2,1,0:T(8,128)}, f32[2,256,512]{2,1,0:T(8,128)S(1)}, u32[]{:S(2)}, u32[]{:S(2)}) collective-permute-start(f32[2,256,512]{2,1,0:T(8,128)} %copy-done.3), channel_id=1, source_target_pairs={{0,8},{8,16},{16,24},{1,9},{9,17},{17,25},{2,10},{10,18},{18,26},{... | collective-permute-start | bytes 3145736 | tf_op jit(solution)/shard_map/ppermute | solution.py:645
  114.6 10.7 %collective-permute-start.8 = (f32[4,64,256]{2,1,0:T(8,128)S(1)}, f32[4,64,256]{2,1,0:T(8,128)S(1)}, u32[]{:S(2)}, u32[]{:S(2)}) collective-permute-start(f32[4,64,256]{2,1,0:T(8,128)S(1)} %collect.1.mine), channel_id=1, source_target_pairs={{0,16},{8,24},{16,0},{24,8},{1,17},{9,25},{17,1},{25,9},{2,18},{10... | collective-permute-start | bytes 786440 | tf_op jit(solution)/shard_map/ppermute | solution.py:650
  118.5 1.0 copy-start.2
  125.8 7.6 %collective-permute-start.9 = (f32[4,128,256]{2,1,0:T(8,128)S(1)}, f32[4,128,256]{2,1,0:T(8,128)S(1)}, u32[]{:S(2)}, u32[]{:S(2)}) collective-permute-start(f32[4,128,256]{2,1,0:T(8,128)S(1)} %join.2.mine), channel_id=1, source_target_pairs={{0,8},{8,0},{16,24},{24,16},{1,9},{9,1},{17,25},{25,17},{2,10},{10... | collective-permute-start | bytes 1572872 | tf_op jit(solution)/shard_map/ppermute | solution.py:650
